TPU v7x, 256 devices: a whole 4x4x8 slice. The times are simulated.
256 devices in a mesh: pair: 128 (over z, y, x), col: 2 (over core).
Axes of the slice: x: 4, y: 4, z: 8, core: 2. Of those that a mesh axis runs over, the one named last changes fastest.
Arguments:
- interferograms: bfloat16 [640, 128, 1024], P('pair', None, 'col'), may hold values from -10 to 10
- coherence: bfloat16 [640, 128, 1024], P('pair', None, 'col'), may hold values from 0.099609375 to 1
- pair_epochs: int32 [640, 2], replicated, may hold values from 0 to 149, as said below
- inverse: bfloat16 [150, 640], replicated, as said below
- footprint: int32 [128, 1024], P('pair', 'col'), may hold values from 0 to 3, as said below
Outputs:
- misfit: float32 [128, 1024], P('pair', 'col')
- volumes: float32 [150, 512], P(None, ('pair', 'col'))
Inputs may be any that keep to these rules, and one draw needn't show every extreme that they name: `pair_epochs`: each row names an earlier and a strictly later epoch; epoch 0 and epoch 150 - 1 both occur. inverse[e, k] = G[k, e] / (1 + the number of interferograms that name epoch e), rounded to bfloat16, where G[k, e] is 1 at later[k], -1 at earlier[k] and 0 elsewhere. `footprint`: offsets place a pixel in its own tile's 2 cells or in the next tile's; the pixels of the last tile of the strip lie in its own cells.
All inputs are finite; a program needn't handle non-finite values.
Results may differ from a plain program's by a relative error of at most 0.0033.
Values may be sent and summed in bfloat16 or wider, within the bound.
No kernel may reach another device: no remote copies, remote signals or barrier semaphores. Data moves between devices by JAX's collectives and lax.ppermute only.
A program may use at most 64 MiB of HBM per device.

v0:
```python
import jax
import jax.numpy as jnp
from jax import lax
from jax.sharding import PartitionSpec as P

PPC = 256
ITERS = 4


phase_scale = 1.5


def from_behind(block, axis, distance):
    devices = range(lax.axis_size(axis))
    route = [(i - distance, i) for i in devices if i - distance in devices]
    return lax.ppermute(block, axis, route)


def residual_weights(motion, phases, quality, earlier, later):
    modeled = jnp.take(motion, later, axis=0) - jnp.take(motion, earlier, axis=0)
    residual = phases - modeled
    weight = quality / (1.0 + (residual / phase_scale) ** 2)
    return (residual, weight)


def reweighted_solve(phase_block, quality_block, pair_epochs, inverse):
    earlier = pair_epochs[:, 0]
    later = pair_epochs[:, 1]
    phases = phase_block.astype(jnp.float32)
    quality = quality_block.astype(jnp.float32)
    motion = jnp.zeros((inverse.shape[0], phase_block.shape[1]), jnp.float32)
    for repeat in range(ITERS):
        residual, weight = residual_weights(motion, phases, quality, earlier, later)
        weighted = (weight * residual).astype(jnp.bfloat16)
        motion = motion + jnp.dot(inverse, weighted, preferred_element_type=jnp.float32)
    residual, weight = residual_weights(motion, phases, quality, earlier, later)
    misfit = jnp.sum(weight * residual * residual, axis=0) / jnp.sum(weight, axis=0)
    return (motion.astype(jnp.bfloat16), misfit[None, :])


def bin_cells(rounded, offsets, window):
    targets = jnp.arange(window, dtype=jnp.int32)
    onehot = (targets[:, None] == offsets[None, :]).astype(jnp.bfloat16)
    return lax.dot_general(
        rounded, onehot, (((1,), (1,)), ((), ())), preferred_element_type=jnp.float32
    )


def body(interferograms, coherence, pair_epochs, inverse, footprint):
    phase_cube = lax.all_to_all(interferograms, "pair", split_axis=1, concat_axis=0, tiled=True)
    quality_cube = lax.all_to_all(coherence, "pair", split_axis=1, concat_axis=0, tiled=True)
    rounded, misfit = reweighted_solve(
        phase_cube[:, 0, :], quality_cube[:, 0, :], pair_epochs, inverse
    )
    tile_pixels = footprint.shape[1]
    cells_tile = tile_pixels // PPC
    partial_value = bin_cells(rounded, footprint[0], 2 * cells_tile)
    own_cells = partial_value[:, :cells_tile]
    spilled = partial_value[:, cells_tile:]
    arrived = from_behind(spilled, ("pair", "col"), 1)
    volumes = own_cells + arrived
    return (misfit, volumes)


def solution(mesh):
    in_specs = (P("pair", None, "col"), P("pair", None, "col"), P(), P(), P("pair", "col"))
    out_specs = (P("pair", "col"), P(None, ("pair", "col")))
    return jax.shard_map(body, mesh=mesh, in_specs=in_specs, out_specs=out_specs, check_vma=False)
```

profile of v0, /device:TPU:32, one launch (start us, length us, event | category | flops | bytes accessed | tf_op | source)
XLA Modules:
  0.0 133.8 jit_solution(5584196590093241257)
XLA Ops:
  0.6 0.0 copy-start
  0.6 2.5 %copy.12 = bf16[5,128,512]{2,0,1:T(8,128)(2,1)} copy(bf16[5,128,512]{2,1,0:T(8,128)(2,1)} %param.7) | data formatting | bytes 1310720 | tf_op args[0]
  3.1 0.0 copy-start.3
  3.1 15.1 %all-to-all-start.1 = ((bf16[5,128,512]{2,0,1:T(8,128)(2,1)}), bf16[5,128,512]{2,0,1:T(8,128)(2,1)S(1)}, u32[]{:S(2)}, u32[]{:S(2)}) async-start(bf16[5,128,512]{2,0,1:T(8,128)(2,1)} %copy.12), calls=%async_computation.1 | async-start | bytes 2097152 | tf_op jit(solution)/shard_map/all_to_all | solution.py:50
  18.3 0.0 copy-done.3
  18.3 1.4 %copy.11 = bf16[5,128,512]{2,0,1:T(8,128)(2,1)} copy(bf16[5,128,512]{2,1,0:T(8,128)(2,1)S(1)} %copy-done.3) | data formatting | bytes 1310720 | tf_op args[1]
  19.6 0.0 copy-start.4
  19.6 30.0 %all-to-all-done.1 = bf16[5,128,512]{2,0,1:T(8,128)(2,1)S(1)} async-done(((bf16[5,128,512]{2,0,1:T(8,128)(2,1)}), bf16[5,128,512]{2,0,1:T(8,128)(2,1)S(1)}, u32[]{:S(2)}, u32[]{:S(2)}) %all-to-all-start.1) | async-done | bytes 655392 | tf_op jit(solution)/shard_map/all_to_all | solution.py:50
  49.6 7.1 %all-to-all-start = ((bf16[5,128,512]{2,0,1:T(8,128)(2,1)}), bf16[5,128,512]{2,0,1:T(8,128)(2,1)}, u32[]{:S(2)}, u32[]{:S(2)}) async-start(bf16[5,128,512]{2,0,1:T(8,128)(2,1)} %copy.11), calls=%async_computation | async-start | bytes 2097152 | tf_op jit(solution)/shard_map/all_to_all | solution.py:51
  56.7 0.0 copy-done.4
  56.8 3.0 %gather_fusion.1 = f32[640,512]{1,0:T(8,128)} fusion(f32[150,512]{1,0:T(8,128)S(1)} %broadcast_in_dim.14, s32[1024]{0:T(1024)S(1)} %pad_clamp_fusion), kind=kCustom, calls=%fused_computation.1.clone | custom fusion | bytes 2624000 | tf_op jit(solution)/shard_map/jit(_take)/gather | solution.py:20
  59.8 3.0 %gather_fusion = f32[640,512]{1,0:T(8,128)} fusion(f32[150,512]{1,0:T(8,128)S(1)} %broadcast_in_dim.14, s32[1024]{0:T(1024)S(1)} %pad_clamp_fusion.1), kind=kCustom, calls=%fused_computation.clone | custom fusion | bytes 2624000 | tf_op jit(solution)/shard_map/jit(_take)/gather | solution.py:20
  62.8 0.3 convert_bitcast_fusion
  63.1 1.3 reshape.32
  64.4 21.9 %all-to-all-done = bf16[5,128,512]{2,0,1:T(8,128)(2,1)} async-done(((bf16[5,128,512]{2,0,1:T(8,128)(2,1)}), bf16[5,128,512]{2,0,1:T(8,128)(2,1)}, u32[]{:S(2)}, u32[]{:S(2)}) %all-to-all-start) | async-done | bytes 655392 | tf_op jit(solution)/shard_map/all_to_all | solution.py:51
  86.4 1.5 %convert_bitcast_fusion.1 = f32[128,5,1,512]{3,1,0,2:T(8,128)S(1)} fusion(bf16[5,128,512]{2,0,1:T(8,128)(2,1)} %all-to-all-done), kind=kLoop, calls=%fused_computation.11 | loop fusion | flops 327680 | bytes 1966080 | tf_op jit(solution)/shard_map/convert_element_type | solution.py:30
  87.9 1.3 reshape.31
  89.2 0.0 copy-done
  89.2 3.2 %convolution_bitcast_fusion.3 = f32[150,512]{1,0:T(8,128)S(1)} fusion(bf16[150,640]{1,0:T(8,128)(2,1)S(1)} %copy-done, f32[640,512]{1,0:T(8,128)} %reshape.31, f32[640,512]{1,0:T(8,128)} %reshape.32, f32[640,512]{1,0:T(8,128)} %gather_fusion.1, f32[640,512]{1,0:T(8,128)} %gather_fusion, pred[640]{0:T(1024)(128)(4,1)S(1)} %get-tuple-element.9, ...), kind=kOutput, calls=%fused_computation.35 | convolution fusion | flops 101580800 | bytes 5743360 | tf_op jit(solution)/shard_map/dot_general | solution.py:35
  92.4 3.0 %gather_fusion.3 = f32[640,512]{1,0:T(8,128)} fusion(f32[150,512]{1,0:T(8,128)S(1)} %convolution_bitcast_fusion.3, s32[1024]{0:T(1024)S(1)} %pad_clamp_fusion), kind=kCustom, calls=%fused_computation.3.clone | custom fusion | bytes 2624000 | tf_op jit(solution)/shard_map/jit(_take)/gather | solution.py:20
  95.5 0.0 copy-start.1
  95.5 0.0 copy-start.2
  95.5 3.0 %gather_fusion.2 = f32[640,512]{1,0:T(8,128)} fusion(f32[150,512]{1,0:T(8,128)S(1)} %convolution_bitcast_fusion.3, s32[1024]{0:T(1024)S(1)} %pad_clamp_fusion.1), kind=kCustom, calls=%fused_computation.2.clone | custom fusion | bytes 2624000 | tf_op jit(solution)/shard_map/jit(_take)/gather | solution.py:20
  98.5 0.0 copy-done.1
  98.5 0.0 copy-done.2
  98.5 2.4 %fusion.8 = f32[150,512]{1,0:T(8,128)S(1)} fusion(f32[150,512]{1,0:T(8,128)S(1)} %convolution_bitcast_fusion.3, bf16[150,640]{1,0:T(8,128)(2,1)S(1)} %copy-done, f32[640,512]{1,0:T(8,128)S(1)} %copy-done.2, f32[640,512]{1,0:T(8,128)S(1)} %copy-done.1, f32[640,512]{1,0:T(8,128)} %gather_fusion.3, f32[640,512]{1,0:T(8,128)} %gather_fusion.2, ...), kind=kOutput, calls=%fused_computation.34 | convolution fusion | flops 101657600 | bytes 6050560 | tf_op jit(solution)/shard_map/dot_general | solution.py:35
  100.9 3.0 %gather_fusion.5 = f32[640,512]{1,0:T(8,128)} fusion(f32[150,512]{1,0:T(8,128)S(1)} %fusion.8, s32[1024]{0:T(1024)S(1)} %pad_clamp_fusion), kind=kCustom, calls=%fused_computation.5.clone | custom fusion | bytes 2624000 | tf_op jit(solution)/shard_map/jit(_take)/gather | solution.py:20
  103.9 3.0 %gather_fusion.4 = f32[640,512]{1,0:T(8,128)} fusion(f32[150,512]{1,0:T(8,128)S(1)} %fusion.8, s32[1024]{0:T(1024)S(1)} %pad_clamp_fusion.1), kind=kCustom, calls=%fused_computation.4.clone | custom fusion | bytes 2624000 | tf_op jit(solution)/shard_map/jit(_take)/gather | solution.py:20
  107.0 2.4 %fusion.7 = f32[150,512]{1,0:T(8,128)S(1)} fusion(f32[150,512]{1,0:T(8,128)S(1)} %fusion.8, bf16[150,640]{1,0:T(8,128)(2,1)S(1)} %copy-done, f32[640,512]{1,0:T(8,128)S(1)} %copy-done.2, f32[640,512]{1,0:T(8,128)S(1)} %copy-done.1, f32[640,512]{1,0:T(8,128)} %gather_fusion.5, f32[640,512]{1,0:T(8,128)} %gather_fusion.4, ...), kind=kOutput, calls=%fused_computation.32 | convolution fusion | flops 101657600 | bytes 6050560 | tf_op jit(solution)/shard_map/dot_general | solution.py:35
  109.4 3.0 %gather_fusion.7 = f32[640,512]{1,0:T(8,128)} fusion(f32[150,512]{1,0:T(8,128)S(1)} %fusion.7, s32[1024]{0:T(1024)S(1)} %pad_clamp_fusion), kind=kCustom, calls=%fused_computation.7.clone | custom fusion | bytes 2624000 | tf_op jit(solution)/shard_map/jit(_take)/gather | solution.py:20
  112.4 3.0 %gather_fusion.6 = f32[640,512]{1,0:T(8,128)} fusion(f32[150,512]{1,0:T(8,128)S(1)} %fusion.7, s32[1024]{0:T(1024)S(1)} %pad_clamp_fusion.1), kind=kCustom, calls=%fused_computation.6.clone | custom fusion | bytes 2624000 | tf_op jit(solution)/shard_map/jit(_take)/gather | solution.py:20
  115.4 2.4 %fusion.6 = f32[150,512]{1,0:T(8,128)S(1)} fusion(f32[150,512]{1,0:T(8,128)S(1)} %fusion.7, bf16[150,640]{1,0:T(8,128)(2,1)S(1)} %copy-done, f32[640,512]{1,0:T(8,128)S(1)} %copy-done.2, f32[640,512]{1,0:T(8,128)S(1)} %copy-done.1, f32[640,512]{1,0:T(8,128)} %gather_fusion.7, f32[640,512]{1,0:T(8,128)} %gather_fusion.6, ...), kind=kOutput, calls=%fused_computation.30 | convolution fusion | flops 101657600 | bytes 6050560 | tf_op jit(solution)/shard_map/dot_general | solution.py:35
  117.9 3.0 %gather_fusion.9 = f32[640,512]{1,0:T(8,128)} fusion(f32[150,512]{1,0:T(8,128)S(1)} %fusion.6, s32[1024]{0:T(1024)S(1)} %pad_clamp_fusion), kind=kCustom, calls=%fused_computation.9.clone | custom fusion | bytes 2624000 | tf_op jit(solution)/shard_map/jit(_take)/gather | solution.py:20
  120.9 0.0 copy-start.5
  120.9 3.0 %gather_fusion.8 = f32[640,512]{1,0:T(8,128)} fusion(f32[150,512]{1,0:T(8,128)S(1)} %fusion.6, s32[1024]{0:T(1024)S(1)} %pad_clamp_fusion.1), kind=kCustom, calls=%fused_computation.8.clone | custom fusion | bytes 2624000 | tf_op jit(solution)/shard_map/jit(_take)/gather | solution.py:20
  123.9 0.0 copy-done.5
  123.9 0.1 fusion.10
  124.1 1.9 %collective-permute-start = (f32[150,2]{0,1:T(2,128)S(1)}, f32[150,2]{0,1:T(2,128)S(1)}, u32[]{:S(2)}, u32[]{:S(2)}) collective-permute-start(f32[150,2]{0,1:T(2,128)S(1)} %slice.37), channel_id=1, source_target_pairs={{0,1},{1,2},{2,3},{3,4},{4,5},{5,6},{6,7},{7,8},{8,9},{9,10},{10,1... | collective-permute-start | bytes 3608 | tf_op jit(solution)/shard_map/ppermute | solution.py:16
  126.0 2.4 %fusion.9 = (f32[512]{0:T(512)S(1)}, f32[512]{0:T(512)S(1)}) fusion(f32[640,512]{1,0:T(8,128)S(1)} %copy-done.2, f32[640,512]{1,0:T(8,128)S(1)} %copy-done.1, f32[640,512]{1,0:T(8,128)} %gather_fusion.9, pred[640]{0:T(1024)(128)(4,1)S(1)} %get-tuple-element.10, f32[640,512]{1,0:T(8,128)} %gather_fusion.8, pred[640]{0:T(1024)(128)(4,1)S(1)} %get-tuple-element.9), kind=kLoop, calls=%fused_computation.36 | loop fusion | flops 3931136 | bytes 5248256 | tf_op jit(solution)/shard_map/reduce_sum | solution.py:37
  128.4 0.6 div.53
  129.0 4.2 %collective-permute-done = f32[150,2]{0,1:T(2,128)S(1)} collective-permute-done((f32[150,2]{0,1:T(2,128)S(1)}, f32[150,2]{0,1:T(2,128)S(1)}, u32[]{:S(2)}, u32[]{:S(2)}) %collective-permute-start) | collective-permute-done | bytes 1232 | tf_op jit(solution)/shard_map/ppermute | solution.py:16
  133.2 0.6 slice_add_fusion
  (7 shorter events, 0.1 us)
Async XLA Ops:
  0.6 88.6 %copy-start = (bf16[150,640]{1,0:T(8,128)(2,1)S(1)}, bf16[150,640]{1,0:T(8,128)(2,1)}, u32[]{:S(2)}) copy-start(bf16[150,640]{1,0:T(8,128)(2,1)} %param.10) | copy-start | bytes 576004
  3.1 15.2 %copy-start.3 = (bf16[5,128,512]{2,1,0:T(8,128)(2,1)S(1)}, bf16[5,128,512]{2,1,0:T(8,128)(2,1)}, u32[]{:S(2)}) copy-start(bf16[5,128,512]{2,1,0:T(8,128)(2,1)} %param.8) | copy-start | bytes 1966084
  3.1 46.5 %all-to-all-start.1 = ((bf16[5,128,512]{2,0,1:T(8,128)(2,1)}), bf16[5,128,512]{2,0,1:T(8,128)(2,1)S(1)}, u32[]{:S(2)}, u32[]{:S(2)}) async-start(bf16[5,128,512]{2,0,1:T(8,128)(2,1)} %copy.12), calls=%async_computation.1 | async-start | bytes 2097152 | tf_op jit(solution)/shard_map/all_to_all | solution.py:50
  19.6 37.0 %copy-start.4 = (s32[640,2]{0,1:T(2,128)S(1)}, s32[640,2]{0,1:T(2,128)}, u32[]{:S(2)}) copy-start(s32[640,2]{0,1:T(2,128)} %param.9) | copy-start | bytes 15364
  49.6 36.8 %all-to-all-start = ((bf16[5,128,512]{2,0,1:T(8,128)(2,1)}), bf16[5,128,512]{2,0,1:T(8,128)(2,1)}, u32[]{:S(2)}, u32[]{:S(2)}) async-start(bf16[5,128,512]{2,0,1:T(8,128)(2,1)} %copy.11), calls=%async_computation | async-start | bytes 2097152 | tf_op jit(solution)/shard_map/all_to_all | solution.py:51
  95.5 3.0 %copy-start.1 = (f32[640,512]{1,0:T(8,128)S(1)}, f32[640,512]{1,0:T(8,128)}, u32[]{:S(2)}) copy-start(f32[640,512]{1,0:T(8,128)} %reshape.32) | copy-start | bytes 3932164
  95.5 3.0 %copy-start.2 = (f32[640,512]{1,0:T(8,128)S(1)}, f32[640,512]{1,0:T(8,128)}, u32[]{:S(2)}) copy-start(f32[640,512]{1,0:T(8,128)} %reshape.31) | copy-start | bytes 3932164
  120.9 3.0 %copy-start.5 = (s32[1,512]{1,0:T(1,128)S(1)}, s32[1,512]{1,0:T(1,128)}, u32[]{:S(2)}) copy-start(s32[1,512]{1,0:T(1,128)} %param.11) | copy-start | bytes 6148
  124.1 9.1 %collective-permute-start = (f32[150,2]{0,1:T(2,128)S(1)}, f32[150,2]{0,1:T(2,128)S(1)}, u32[]{:S(2)}, u32[]{:S(2)}) collective-permute-start(f32[150,2]{0,1:T(2,128)S(1)} %slice.37), channel_id=1, source_target_pairs={{0,1},{1,2},{2,3},{3,4},{4,5},{5,6},{6,7},{7,8},{8,9},{9,10},{10,1... | collective-permute-start | bytes 3608 | tf_op jit(solution)/shard_map/ppermute | solution.py:16
where the time goes:
time: 134 us
  waiting for transfers between devices  56.1 us (42%)
  local copies, waits for them, and re-layouts  36.7 us (27%)
  starting transfers between devices  24.1 us (18%)
  matrix products  10.7 us (8%)
  other arithmetic  5.34 us (4%)
    all_to_all x1, waiting for transfers between devices, body(): lax.all_to_all(interferograms, 'pair', split_axis=1, concat_axis=0, tiled...  30 us
    all_to_all x1, waiting for transfers between devices, body(): lax.all_to_all(coherence, 'pair', split_axis=1, concat_axis=0, tiled=True)  21.9 us
    all_to_all x1, starting transfers between devices, body(): lax.all_to_all(interferograms, 'pair', split_axis=1, concat_axis=0, tiled...  15.1 us
    gather x5, local copies, waits for them, and re-layouts, residual_weights(): jnp.take(motion, later, axis=0) - jnp.take(motion, earlier, axis=0)  15.1 us
    gather x5, local copies, waits for them, and re-layouts, residual_weights(): jnp.take(motion, earlier, axis=0)  15.1 us
    dot_general x4, matrix products, reweighted_solve(): jnp.dot(inverse, weighted, preferred_element_type=jnp.float32)  10.5 us
    all_to_all x1, starting transfers between devices, body(): lax.all_to_all(coherence, 'pair', split_axis=1, concat_axis=0, tiled=True)  7.06 us
    ppermute x1, waiting for transfers between devices, from_behind(): return lax.ppermute(block, axis, route)  4.23 us
  transfers between devices with their start and end apart: 3, of which 3 were waited for; matrix products, arithmetic and copies ran while one was open for 9% of the time, Pallas kernels for 0%

commit v1 on v0

v1 whole, which is shorter than its diff:
```python
import functools

import jax
import jax.numpy as jnp
from jax import lax
from jax.experimental import pallas as pl
from jax.experimental.pallas import tpu as pltpu
from jax.sharding import PartitionSpec as P

PPC = 256
ITERS = 4
LANES = 128
SUBLANES = 8
EPOCH_ROWS = 160
EPOCH_DEPTH = 256

phase_scale = 1.5
scale_squared = phase_scale**2


def from_behind(block, axis, distance):
    devices = range(lax.axis_size(axis))
    route = [(i - distance, i) for i in devices if i - distance in devices]
    return lax.ppermute(block, axis, route)


def pack_kernel(phase_ref, quality_ref, packed_ref, rows_ref):
    pairs, slabs, pixels = phase_ref.shape
    chunks = pixels // LANES
    block = pairs * 2 * chunks
    for group in range(slabs // 16):
        for k in range(pairs):
            for which, ref in enumerate((phase_ref, quality_ref)):
                for c in range(chunks):
                    tile = ref[k, pl.ds(group * 16, 16), pl.ds(c * LANES, LANES)].astype(jnp.float32)
                    row = k * 2 * chunks + which * chunks + c
                    for half in range(2):
                        first = (group * 16 + half * 8) * block + row
                        rows_ref[pl.ds(first, 8, stride=block), :] = tile[half * 8 : half * 8 + 8]
    for at in range(0, slabs * block, 16):
        packed_ref[pl.ds(at, 16), :] = rows_ref[pl.ds(at, 16), :].astype(jnp.bfloat16)


def pack(interferograms, coherence):
    pairs, slabs, pixels = interferograms.shape
    rows = slabs * pairs * 2 * pixels // LANES
    return pl.pallas_call(
        pack_kernel,
        out_shape=jax.ShapeDtypeStruct((rows, LANES), jnp.bfloat16),
        in_specs=[pl.BlockSpec(memory_space=pltpu.VMEM)] * 2,
        out_specs=pl.BlockSpec(memory_space=pltpu.VMEM),
        scratch_shapes=[pltpu.VMEM((rows, LANES), jnp.float32)],
        compiler_params=pltpu.CompilerParams(vmem_limit_bytes=16 << 20),
        name="pack",
    )(interferograms, coherence)


def prepare_kernel(named_ref, inverse_ref, design_ref, spread_ref):
    pairs = named_ref.shape[1]
    epochs = lax.broadcasted_iota(jnp.int32, (EPOCH_DEPTH, pairs), 0)
    later = (epochs == named_ref[1:2, :]).astype(jnp.float32)
    earlier = (epochs == named_ref[0:1, :]).astype(jnp.float32)
    design_ref[...] = (later - earlier).T.astype(jnp.bfloat16)
    spread_ref[...] = jnp.zeros_like(spread_ref)
    spread_ref[0 : inverse_ref.shape[0], :] = inverse_ref[...]


def prepare(pair_epochs, inverse):
    pairs = pair_epochs.shape[0]
    return pl.pallas_call(
        prepare_kernel,
        out_shape=(
            jax.ShapeDtypeStruct((pairs, EPOCH_DEPTH), jnp.bfloat16),
            jax.ShapeDtypeStruct((EPOCH_ROWS, pairs), jnp.bfloat16),
        ),
        in_specs=[pl.BlockSpec(memory_space=pltpu.VMEM)] * 2,
        out_specs=[pl.BlockSpec(memory_space=pltpu.VMEM)] * 2,
        compiler_params=pltpu.CompilerParams(vmem_limit_bytes=16 << 20),
        name="prepare",
    )(pair_epochs.T, inverse)


def solve_kernel(
    received_ref, design_ref, spread_ref, footprint_ref, misfit_ref, cells_ref,
    rows_ref, phase_ref, quality_ref, motion_ref, high_ref, low_ref,
):
    pairs, pixels = phase_ref.shape
    chunks = pixels // LANES
    deep = 128
    for at in range(0, rows_ref.shape[0], 16):
        rows_ref[pl.ds(at, 16), :] = received_ref[pl.ds(at, 16), :].astype(jnp.float32)

    def first_block(k0):
        parts = []
        for c in range(chunks):
            column = []
            for k in range(k0, k0 + deep, 8):
                phase = rows_ref[pl.ds(k * 8 + c, 8, stride=8), :]
                quality = rows_ref[pl.ds(k * 8 + chunks + c, 8, stride=8), :] * scale_squared
                phase_ref[pl.ds(k, 8), pl.ds(c * LANES, LANES)] = phase
                quality_ref[pl.ds(k, 8), pl.ds(c * LANES, LANES)] = quality
                column.append(quality * phase / (scale_squared + phase * phase))
            parts.append(jnp.concatenate(column, axis=0))
        return jnp.concatenate(parts, axis=1).astype(jnp.bfloat16)

    def modeled(k0):
        design = design_ref[pl.ds(k0, deep), :]
        return jnp.dot(design, high_ref[...], preferred_element_type=jnp.float32) + jnp.dot(
            design, low_ref[...], preferred_element_type=jnp.float32
        )

    def block_weights(k0):
        residual = phase_ref[pl.ds(k0, deep), :] - modeled(k0)
        square = residual * residual
        weight = quality_ref[pl.ds(k0, deep), :] / (scale_squared + square)
        return residual, square, weight

    def keep(motion):
        motion_ref[...] = motion
        high = motion.astype(jnp.bfloat16)
        high_ref[0:EPOCH_ROWS, :] = high
        low_ref[0:EPOCH_ROWS, :] = (motion - high.astype(jnp.float32)).astype(jnp.bfloat16)

    high_ref[...] = jnp.zeros_like(high_ref)
    low_ref[...] = jnp.zeros_like(low_ref)
    for repeat in range(ITERS):
        change = jnp.zeros((EPOCH_ROWS, pixels), jnp.float32)
        for k0 in range(0, pairs, deep):
            if repeat == 0:
                weighted = first_block(k0)
            else:
                residual, _, weight = block_weights(k0)
                weighted = (weight * residual).astype(jnp.bfloat16)
            change += jnp.dot(
                spread_ref[:, pl.ds(k0, deep)], weighted, preferred_element_type=jnp.float32
            )
        keep(change if repeat == 0 else motion_ref[...] + change)

    targets = lax.broadcasted_iota(jnp.int32, (SUBLANES, pixels), 0)
    onehot = (targets == footprint_ref[...]).astype(jnp.bfloat16)
    cells_ref[...] = lax.dot_general(
        onehot, high_ref[...], (((1,), (1,)), ((), ())), preferred_element_type=jnp.float32
    )

    above = jnp.zeros((SUBLANES, pixels), jnp.float32)
    below = jnp.zeros((SUBLANES, pixels), jnp.float32)
    for k0 in range(0, pairs, deep):
        _, square, weight = block_weights(k0)
        above += jnp.sum((weight * square).reshape(deep // 8, 8, pixels), axis=0)
        below += jnp.sum(weight.reshape(deep // 8, 8, pixels), axis=0)
    misfit_ref[...] = jnp.sum(above, axis=0, keepdims=True) / jnp.sum(below, axis=0, keepdims=True)


def solve(received, design, spread, footprint):
    pairs = design.shape[0]
    pixels = footprint.shape[1]
    return pl.pallas_call(
        solve_kernel,
        out_shape=(
            jax.ShapeDtypeStruct((1, pixels), jnp.float32),
            jax.ShapeDtypeStruct((SUBLANES, EPOCH_DEPTH), jnp.float32),
        ),
        in_specs=[pl.BlockSpec(memory_space=pltpu.VMEM)] * 4,
        out_specs=[pl.BlockSpec(memory_space=pltpu.VMEM)] * 2,
        scratch_shapes=[
            pltpu.VMEM(received.shape, jnp.float32),
            pltpu.VMEM((pairs, pixels), jnp.float32),
            pltpu.VMEM((pairs, pixels), jnp.float32),
            pltpu.VMEM((EPOCH_ROWS, pixels), jnp.float32),
            pltpu.VMEM((EPOCH_DEPTH, pixels), jnp.bfloat16),
            pltpu.VMEM((EPOCH_DEPTH, pixels), jnp.bfloat16),
        ],
        compiler_params=pltpu.CompilerParams(vmem_limit_bytes=24 << 20),
        name="solve",
    )(received, design, spread, footprint)


def body(interferograms, coherence, pair_epochs, inverse, footprint):
    slabs = lax.axis_size("pair")
    packed = pack(interferograms, coherence)
    blocks = packed.reshape(slabs, packed.shape[0] // slabs, LANES)
    blocks = lax.all_to_all(blocks, "pair", split_axis=0, concat_axis=0, tiled=True)
    received = blocks.reshape(packed.shape)
    design, spread = prepare(pair_epochs, inverse)
    misfit, cells = solve(received, design, spread, footprint)
    cells_tile = footprint.shape[1] // PPC
    epochs = inverse.shape[0]
    own_cells = cells[:cells_tile, :epochs]
    spilled = cells[cells_tile : 2 * cells_tile, :epochs]
    arrived = from_behind(spilled, ("pair", "col"), 1)
    return (misfit, (own_cells + arrived).T)


def solution(mesh):
    in_specs = (P("pair", None, "col"), P("pair", None, "col"), P(), P(), P("pair", "col"))
    out_specs = (P("pair", "col"), P(None, ("pair", "col")))
    return jax.shard_map(body, mesh=mesh, in_specs=in_specs, out_specs=out_specs, check_vma=False)
```

time: 134 us -> 72.5 us (0.54)
  local copies, waits for them, and re-layouts: 36.7 us -> 2.18 us
  waiting for transfers between devices: 56.1 us -> 43.8 us
  matrix products: 10.7 us -> 0 us
  Pallas kernels: 0 us -> 7.93 us
  starting transfers between devices: 24.1 us -> 17.1 us
  other arithmetic: 5.34 us -> 0.58 us
    gather x10 -> x0, local copies, waits for them, and re-layouts: 30.2 us -> none  [the longest x5 15.1 us: residual_weights(): jnp.take(motion, later, axis=0) - jnp.take(motion, earlier, axis=0)]
    all_to_all x2 -> x1, waiting for transfers between devices: 51.9 us -> 36.6 us  [body(): lax.all_to_all(blocks, 'pair', split_axis=0, concat_axis=0, tiled=True)]
    dot_general x5 -> x0, matrix products: 10.7 us -> none  [the longest x4 10.5 us: reweighted_solve(): jnp.dot(inverse, weighted, preferred_element_type=jnp.float32)]
    pallas_call x0 -> x3, Pallas kernels: none -> 7.93 us  [the longest x1 6.15 us: solve(): pl.pallas_call(solve_kernel, out_shape=(jax.ShapeDtypeStruct((1, pixels),...]
    all_to_all x2 -> x1, starting transfers between devices: 22.2 us -> 15.1 us  [body(): lax.all_to_all(blocks, 'pair', split_axis=0, concat_axis=0, tiled=True)]
    ppermute x1, waiting for transfers between devices: 4.23 us -> 7.19 us  [from_behind(): return lax.ppermute(block, axis, route)]
    convert_element_type x2 -> x0, local copies, waits for them, and re-layouts: 2.62 us -> none  [the longest x1 1.32 us: reweighted_solve(): quality = quality_block.astype(jnp.float32)]
    reduce_sum x1 -> x0, other arithmetic: 2.37 us -> none  [reweighted_solve(): jnp.sum(weight, axis=0)]
  transfers between devices with their start and end apart: 3 -> 2, of which waited for: 3 -> 2; matrix products, arithmetic and copies ran while one was open for 9% -> 0% of each run, Pallas kernels for 0% -> 0%
where the time goes in v1:
time: 72.5 us; the launch traced here: 72.3 us
  waiting for transfers between devices  43.8 us (60%)
  starting transfers between devices  17.1 us (24%)
  Pallas kernels  7.93 us (11%)
  local copies, waits for them, and re-layouts  2.18 us (3%)
    all_to_all x1, waiting for transfers between devices, body(): lax.all_to_all(blocks, 'pair', split_axis=0, concat_axis=0, tiled=True)  36.6 us
    all_to_all x1, starting transfers between devices, body(): lax.all_to_all(blocks, 'pair', split_axis=0, concat_axis=0, tiled=True)  15.1 us
    ppermute x1, waiting for transfers between devices, from_behind(): return lax.ppermute(block, axis, route)  7.19 us
    pallas_call x1, Pallas kernels, solve(): pl.pallas_call(solve_kernel, out_shape=(jax.ShapeDtypeStruct((1, pixels),...  6.15 us
    unnamed x10, local copies, waits for them, and re-layouts  2.18 us
    ppermute x1, starting transfers between devices, from_behind(): return lax.ppermute(block, axis, route)  1.91 us
    pallas_call x1, Pallas kernels, pack(): pl.pallas_call(pack_kernel, out_shape=jax.ShapeDtypeStruct((rows, LANES),...  1.57 us
  transfers between devices with their start and end apart: 2, of which 2 were waited for; matrix products, arithmetic and copies ran while one was open for 0% of the time, Pallas kernels for 0%

profile of v1, /device:TPU:32, one launch (start us, length us, event | category | flops | bytes accessed | tf_op | source)
XLA Modules:
  0.0 72.3 jit_solution(10829827677262295678)
XLA Ops:
  0.6 0.0 copy-start
  0.6 1.1 %copy-done = bf16[5,128,512]{2,1,0:T(8,128)(2,1)S(1)} copy-done((bf16[5,128,512]{2,1,0:T(8,128)(2,1)S(1)}, bf16[5,128,512]{2,1,0:T(8,128)(2,1)}, u32[]{:S(2)}) %copy-start) | copy-done | bytes 655384
  1.7 0.0 copy-start.1
  1.7 1.1 %copy-done.1 = bf16[5,128,512]{2,1,0:T(8,128)(2,1)S(1)} copy-done((bf16[5,128,512]{2,1,0:T(8,128)(2,1)S(1)}, bf16[5,128,512]{2,1,0:T(8,128)(2,1)}, u32[]{:S(2)}) %copy-start.1) | copy-done | bytes 655384
  2.8 1.6 %pack.1 = bf16[5120,128]{1,0:T(8,128)(2,1)} custom-call(bf16[5,128,512]{2,1,0:T(8,128)(2,1)S(1)} %copy-done, bf16[5,128,512]{2,1,0:T(8,128)(2,1)S(1)} %copy-done.1), custom_call_target="tpu_custom_call" | custom-call | tf_op jit(solution)/shard_map/pack/pallas_call | solution.py:47
  4.4 0.0 copy-start.2
  4.4 0.0 copy-start.3
  4.4 0.0 copy-start.4
  4.4 15.1 %all-to-all-start = ((bf16[128,40,128]{2,1,0:T(8,128)(2,1)}), bf16[128,40,128]{2,1,0:T(8,128)(2,1)S(1)}, u32[]{:S(2)}, u32[]{:S(2)}) async-start(bf16[128,40,128]{2,1,0:T(8,128)(2,1)} %bitcast), calls=%async_computation | async-start | bytes 2621440 | tf_op jit(solution)/shard_map/all_to_all | solution.py:182
  19.5 0.0 copy-done.2
  19.5 0.0 copy-done.3
  19.6 0.2 prepare.1
  19.8 36.6 %all-to-all-done = bf16[128,40,128]{2,1,0:T(8,128)(2,1)S(1)} async-done(((bf16[128,40,128]{2,1,0:T(8,128)(2,1)}), bf16[128,40,128]{2,1,0:T(8,128)(2,1)S(1)}, u32[]{:S(2)}, u32[]{:S(2)}) %all-to-all-start) | async-done | bytes 1310752 | tf_op jit(solution)/shard_map/all_to_all | solution.py:182
  56.4 0.0 copy-done.4
  56.4 6.2 %solve.1 = (f32[1,512]{1,0:T(1,128)}, f32[8,256]{1,0:T(8,128)S(1)}) custom-call(bf16[5120,128]{1,0:T(8,128)(2,1)S(1)} %bitcast.5, bf16[640,256]{1,0:T(8,128)(2,1)S(1)} %get-tuple-element.6.design_ref, bf16[160,640]{1,0:T(8,128)(2,1)S(1)} %get-tuple-element.7.spread_ref, s32[1,512]{1,0:T(1,128)S(1)} %copy-done.4), custom_call_target="tpu_custom_call" | custom-call | tf_op jit(solution)/shard_map/solve/pallas_call | solution.py:157
  62.6 1.9 %collective-permute-start = (f32[2,150]{1,0:T(2,128)S(1)}, f32[2,150]{1,0:T(2,128)S(1)}, u32[]{:S(2)}, u32[]{:S(2)}) collective-permute-start(f32[2,150]{1,0:T(2,128)S(1)} %slice.7), channel_id=1, source_target_pairs={{0,1},{1,2},{2,3},{3,4},{4,5},{5,6},{6,7},{7,8},{8,9},{9,10},{10,1... | collective-permute-start | bytes 3608 | tf_op jit(solution)/shard_map/ppermute | solution.py:24
  64.5 7.2 %collective-permute-done = f32[2,150]{1,0:T(2,128)S(1)} collective-permute-done((f32[2,150]{1,0:T(2,128)S(1)}, f32[2,150]{1,0:T(2,128)S(1)}, u32[]{:S(2)}, u32[]{:S(2)}) %collective-permute-start) | collective-permute-done | bytes 1232 | tf_op jit(solution)/shard_map/ppermute | solution.py:24
  71.7 0.6 add_bitcast_fusion
  (1 shorter events, 0.0 us)
Async XLA Ops:
  0.6 1.1 %copy-start = (bf16[5,128,512]{2,1,0:T(8,128)(2,1)S(1)}, bf16[5,128,512]{2,1,0:T(8,128)(2,1)}, u32[]{:S(2)}) copy-start(bf16[5,128,512]{2,1,0:T(8,128)(2,1)} %phase_ref.1) | copy-start | bytes 1966084
  1.7 1.1 %copy-start.1 = (bf16[5,128,512]{2,1,0:T(8,128)(2,1)S(1)}, bf16[5,128,512]{2,1,0:T(8,128)(2,1)}, u32[]{:S(2)}) copy-start(bf16[5,128,512]{2,1,0:T(8,128)(2,1)} %quality_ref.1) | copy-start | bytes 1966084
  4.4 15.2 %copy-start.2 = (bf16[150,640]{1,0:T(8,128)(2,1)S(1)}, bf16[150,640]{1,0:T(8,128)(2,1)}, u32[]{:S(2)}) copy-start(bf16[150,640]{1,0:T(8,128)(2,1)} %inverse_ref.1) | copy-start | bytes 576004
  4.4 15.2 %copy-start.3 = (s32[640,2]{0,1:T(2,128)S(1)}, s32[640,2]{0,1:T(2,128)}, u32[]{:S(2)}) copy-start(s32[640,2]{0,1:T(2,128)} %param.7) | copy-start | bytes 15364
  4.4 52.0 %copy-start.4 = (s32[1,512]{1,0:T(1,128)S(1)}, s32[1,512]{1,0:T(1,128)}, u32[]{:S(2)}) copy-start(s32[1,512]{1,0:T(1,128)} %footprint_ref.1) | copy-start | bytes 6148
  4.4 52.0 %all-to-all-start = ((bf16[128,40,128]{2,1,0:T(8,128)(2,1)}), bf16[128,40,128]{2,1,0:T(8,128)(2,1)S(1)}, u32[]{:S(2)}, u32[]{:S(2)}) async-start(bf16[128,40,128]{2,1,0:T(8,128)(2,1)} %bitcast), calls=%async_computation | async-start | bytes 2621440 | tf_op jit(solution)/shard_map/all_to_all | solution.py:182
  62.6 9.1 %collective-permute-start = (f32[2,150]{1,0:T(2,128)S(1)}, f32[2,150]{1,0:T(2,128)S(1)}, u32[]{:S(2)}, u32[]{:S(2)}) collective-permute-start(f32[2,150]{1,0:T(2,128)S(1)} %slice.7), channel_id=1, source_target_pairs={{0,1},{1,2},{2,3},{3,4},{4,5},{5,6},{6,7},{7,8},{8,9},{9,10},{10,1... | collective-permute-start | bytes 3608 | tf_op jit(solution)/shard_map/ppermute | solution.py:24

commit v2 on v0

v2 whole, which is shorter than its diff:
```python
import jax
import jax.numpy as jnp
import numpy as np
from jax import lax
from jax.experimental import pallas as pl
from jax.experimental.pallas import tpu as pltpu
from jax.sharding import PartitionSpec as P

PPC = 256
ITERS = 4
LANES = 128
SUBLANES = 8
GROUP = 16
EPOCH_ROWS = 160
EPOCH_DEPTH = 256
HALF = 256
ORDER_SEED = 102

phase_scale = 1.5
scale_squared = phase_scale**2

VMEM = pl.BlockSpec(memory_space=pltpu.VMEM)
HBM = pl.BlockSpec(memory_space=pltpu.HBM)


def exchange_order(devices):
    halves = np.random.RandomState(ORDER_SEED).permutation(devices // 2)
    return [int(2 * half + side) for half in halves for side in range(2)]


def from_behind(block, axis, distance):
    devices = range(lax.axis_size(axis))
    route = [(i - distance, i) for i in devices if i - distance in devices]
    return lax.ppermute(block, axis, route)


def swap_rows(outer, scale_late):
    inner = LANES // outer
    row = lax.broadcasted_iota(jnp.int32, (LANES, LANES), 0)
    column = lax.broadcasted_iota(jnp.int32, (LANES, LANES), 1)
    hit = (row // inner == column % outer) & (row % inner == column // outer)
    value = jnp.where(row >= LANES // 2, scale_late, 1.0)
    return jnp.where(hit, value, 0.0).astype(jnp.bfloat16)


def pack_kernel(order, phase_hbm, quality_hbm, packed_ref, phase_ref, quality_ref, sems):
    pairs, slabs, pixels = phase_ref.shape
    step = slabs // sems.shape[0]
    copies = []
    for part in range(sems.shape[0]):
        for which, (source, target) in enumerate(((phase_hbm, phase_ref), (quality_hbm, quality_ref))):
            span = pl.ds(part * step, step)
            copies.append(
                pltpu.make_async_copy(source.at[:, span, :], target.at[:, span, :], sems.at[part, which])
            )
            copies[-1].start()
    place = {slab: at for at, slab in enumerate(order)}
    swap = swap_rows(GROUP, 1.0)
    for group in range(slabs // GROUP):
        if group * GROUP % step == 0:
            for copy in copies[2 * (group * GROUP // step) :][:2]:
                copy.wait()
        rows = [
            jnp.concatenate(
                [ref[k, pl.ds(group * GROUP, GROUP), pl.ds(c * LANES, LANES)] for k in range(pairs)], axis=1
            )
            for ref in (phase_ref, quality_ref)
            for c in range(pixels // LANES)
        ]
        swapped = jnp.dot(swap, jnp.concatenate(rows, axis=0), preferred_element_type=jnp.float32)
        for slab in range(0, GROUP, 2):
            tiles = [
                swapped[s * SUBLANES : (s + 1) * SUBLANES, k * LANES : (k + 1) * LANES]
                for s in (slab, slab + 1)
                for k in range(pairs)
            ]
            first = place[group * GROUP + slab] * pairs * SUBLANES
            for at in range(0, len(tiles), 2):
                packed_ref[pl.ds(first + at * SUBLANES, 2 * SUBLANES), :] = jnp.concatenate(
                    tiles[at : at + 2], axis=0
                ).astype(jnp.bfloat16)


def pack(interferograms, coherence, order):
    pairs, slabs, pixels = interferograms.shape
    rows = slabs * pairs * 2 * pixels // LANES
    return pl.pallas_call(
        lambda *refs: pack_kernel(order, *refs),
        out_shape=jax.ShapeDtypeStruct((rows, LANES), jnp.bfloat16),
        in_specs=[HBM] * 2,
        out_specs=VMEM,
        scratch_shapes=[
            pltpu.VMEM(interferograms.shape, jnp.bfloat16),
            pltpu.VMEM(coherence.shape, jnp.bfloat16),
            pltpu.SemaphoreType.DMA((2, 2)),
        ],
        compiler_params=pltpu.CompilerParams(vmem_limit_bytes=60 << 20),
        name="pack",
    )(interferograms, coherence)


def prepare_kernel(arrival_ref, named_ref, inverse_ref, design_ref, spread_ref):
    pairs = named_ref.shape[1]
    reorder = (lax.broadcasted_iota(jnp.int32, (pairs, pairs), 0) == arrival_ref[...]).astype(jnp.bfloat16)
    named = jnp.dot(
        named_ref[...].astype(jnp.float32).astype(jnp.bfloat16), reorder, preferred_element_type=jnp.float32
    )
    epochs = lax.broadcasted_iota(jnp.int32, (EPOCH_DEPTH, pairs), 0).astype(jnp.float32)
    later = (epochs == named[1:2, :]).astype(jnp.float32)
    earlier = (epochs == named[0:1, :]).astype(jnp.float32)
    design = (later - earlier).T.astype(jnp.bfloat16)
    design_ref[:, 0:EPOCH_DEPTH] = design
    design_ref[:, EPOCH_DEPTH:] = design
    spread = jnp.dot(inverse_ref[...], reorder, preferred_element_type=jnp.float32).astype(jnp.bfloat16)
    spread_ref[...] = jnp.zeros_like(spread_ref)
    spread_ref[0 : inverse_ref.shape[0], :] = spread


def prepare(pair_epochs, inverse, arrival):
    pairs = pair_epochs.shape[0]
    return pl.pallas_call(
        prepare_kernel,
        out_shape=(
            jax.ShapeDtypeStruct((pairs, 2 * EPOCH_DEPTH), jnp.bfloat16),
            jax.ShapeDtypeStruct((EPOCH_ROWS, pairs), jnp.bfloat16),
        ),
        in_specs=[VMEM] * 3,
        out_specs=[VMEM] * 2,
        compiler_params=pltpu.CompilerParams(vmem_limit_bytes=16 << 20),
        name="prepare",
    )(arrival, pair_epochs.T, inverse)


def sweeps_kernel(
    received_ref, design_ref, spread_ref, footprint_ref, cells_ref, phase_ref, quality_ref, parts_ref,
    motion_ref, weighted_ref, modeled_ref,
):
    pairs, pixels = phase_ref.shape
    chunks = pixels // LANES
    swap = swap_rows(SUBLANES, scale_squared)
    for group in range(0, pairs // GROUP, 2):
        taken = [received_ref[pl.ds((group + side) * LANES, LANES), :] for side in range(2)]
        swapped = jnp.dot(swap, jnp.concatenate(taken, axis=1), preferred_element_type=jnp.float32)
        for side in range(2):
            lanes = swapped[:, side * LANES : (side + 1) * LANES]
            for c in range(chunks):
                rows, columns = pl.ds((group + side) * GROUP, GROUP), pl.ds(c * LANES, LANES)
                phase = lanes[c * GROUP : (c + 1) * GROUP]
                quality = lanes[(chunks + c) * GROUP : (chunks + c + 1) * GROUP]
                phase_ref[rows, columns] = phase
                quality_ref[rows, columns] = quality
                weighted_ref[rows, columns] = (quality * phase / (scale_squared + phase * phase)).astype(
                    jnp.bfloat16
                )
    parts_ref[...] = jnp.zeros_like(parts_ref)
    for repeat in range(ITERS):
        for half in range(0, pixels, HALF):
            columns = pl.ds(half, HALF)
            if repeat > 0:
                for k in range(0, pairs, LANES):
                    rows = pl.ds(k, LANES)
                    residual = phase_ref[rows, columns] - modeled_ref[rows, columns]
                    weighted_ref[rows, columns] = (
                        quality_ref[rows, columns] * residual / (scale_squared + residual * residual)
                    ).astype(jnp.bfloat16)
            motion = jnp.dot(spread_ref[...], weighted_ref[:, columns], preferred_element_type=jnp.float32)
            if repeat > 0:
                motion = motion_ref[:, columns] + motion
            motion_ref[:, columns] = motion
            high = motion.astype(jnp.bfloat16)
            parts_ref[0:EPOCH_ROWS, columns] = high
            parts_ref[EPOCH_DEPTH : EPOCH_DEPTH + EPOCH_ROWS, columns] = (
                motion - high.astype(jnp.float32)
            ).astype(jnp.bfloat16)
            if repeat < ITERS - 1:
                modeled_ref[:, columns] = jnp.dot(
                    design_ref[...], parts_ref[:, columns], preferred_element_type=jnp.float32
                )
    targets = lax.broadcasted_iota(jnp.int32, (SUBLANES, pixels), 0)
    onehot = (targets == footprint_ref[...]).astype(jnp.bfloat16)
    cells_ref[...] = lax.dot_general(
        onehot, parts_ref[0:EPOCH_DEPTH, :], (((1,), (1,)), ((), ())), preferred_element_type=jnp.float32
    )


def sweeps(received, design, spread, footprint):
    pairs = design.shape[0]
    pixels = footprint.shape[1]
    return pl.pallas_call(
        sweeps_kernel,
        out_shape=(
            jax.ShapeDtypeStruct((SUBLANES, EPOCH_DEPTH), jnp.float32),
            jax.ShapeDtypeStruct((pairs, pixels), jnp.float32),
            jax.ShapeDtypeStruct((pairs, pixels), jnp.float32),
            jax.ShapeDtypeStruct((2 * EPOCH_DEPTH, pixels), jnp.bfloat16),
        ),
        in_specs=[VMEM] * 4,
        out_specs=[VMEM] * 4,
        scratch_shapes=[
            pltpu.VMEM((EPOCH_ROWS, pixels), jnp.float32),
            pltpu.VMEM((pairs, pixels), jnp.bfloat16),
            pltpu.VMEM((pairs, pixels), jnp.float32),
        ],
        compiler_params=pltpu.CompilerParams(vmem_limit_bytes=24 << 20),
        name="sweeps",
    )(received, design, spread, footprint)


def misfit_kernel(design_ref, phase_ref, quality_ref, parts_ref, misfit_ref, modeled_ref):
    pairs, pixels = phase_ref.shape
    for half in range(0, pixels, HALF):
        columns = pl.ds(half, HALF)
        modeled_ref[:, columns] = jnp.dot(
            design_ref[...], parts_ref[:, columns], preferred_element_type=jnp.float32
        )
    for half in range(0, pixels, HALF):
        columns = pl.ds(half, HALF)
        above = jnp.zeros((SUBLANES, HALF), jnp.float32)
        below = jnp.zeros((SUBLANES, HALF), jnp.float32)
        for k in range(0, pairs, SUBLANES):
            rows = pl.ds(k, SUBLANES)
            residual = phase_ref[rows, columns] - modeled_ref[rows, columns]
            square = residual * residual
            weight = quality_ref[rows, columns] / (scale_squared + square)
            above += weight * square
            below += weight
        misfit_ref[:, columns] = jnp.sum(above, axis=0, keepdims=True) / jnp.sum(below, axis=0, keepdims=True)


def misfits(design, phase, quality, parts):
    pairs, pixels = phase.shape
    return pl.pallas_call(
        misfit_kernel,
        out_shape=jax.ShapeDtypeStruct((1, pixels), jnp.float32),
        in_specs=[VMEM] * 4,
        out_specs=VMEM,
        scratch_shapes=[pltpu.VMEM((pairs, pixels), jnp.float32)],
        compiler_params=pltpu.CompilerParams(vmem_limit_bytes=24 << 20),
        name="misfit",
    )(design, phase, quality, parts)


def body(interferograms, coherence, pair_epochs, inverse, footprint):
    devices = lax.axis_size("pair")
    order = exchange_order(devices)
    packed = pack(interferograms, coherence, order)
    blocks = lax.all_to_all(
        packed.reshape(devices, packed.shape[0] // devices, LANES),
        "pair",
        split_axis=0,
        concat_axis=0,
        tiled=True,
        axis_index_groups=[order],
    )
    local = interferograms.shape[0]
    arrival = np.array([[device * local + k for device in order for k in range(local)]], np.int32)
    design, spread = prepare(pair_epochs, inverse, jnp.asarray(arrival))
    cells, phase, quality, parts = sweeps(blocks.reshape(packed.shape), design, spread, footprint)
    cells_tile = footprint.shape[1] // PPC
    epochs = inverse.shape[0]
    own_cells = cells[:cells_tile, :epochs]
    spilled = cells[cells_tile : 2 * cells_tile, :epochs]
    arrived = from_behind(spilled, ("pair", "col"), 1)
    misfit = misfits(design, phase, quality, parts)
    return (misfit, (own_cells + arrived).T)


def solution(mesh):
    in_specs = (P("pair", None, "col"), P("pair", None, "col"), P(), P(), P("pair", "col"))
    out_specs = (P("pair", "col"), P(None, ("pair", "col")))
    return jax.shard_map(body, mesh=mesh, in_specs=in_specs, out_specs=out_specs, check_vma=False)
```

time: 134 us -> 62.9 us (0.47)
  local copies, waits for them, and re-layouts: 36.7 us -> 0.03 us
  waiting for transfers between devices: 56.1 us -> 34 us
  matrix products: 10.7 us -> 0 us
  Pallas kernels: 0 us -> 7.83 us
  other arithmetic: 5.34 us -> 0.58 us
  starting transfers between devices: 24.1 us -> 19.5 us
    gather x10 -> x0, local copies, waits for them, and re-layouts: 30.2 us -> none  [the longest x5 15.1 us: residual_weights(): jnp.take(motion, later, axis=0) - jnp.take(motion, earlier, axis=0)]
    all_to_all x2 -> x1, waiting for transfers between devices: 51.9 us -> 28.1 us  [body(): lax.all_to_all(packed.reshape(devices, packed.shape[0] // devices, LANES)...]
    dot_general x5 -> x0, matrix products: 10.7 us -> none  [the longest x4 10.5 us: reweighted_solve(): jnp.dot(inverse, weighted, preferred_element_type=jnp.float32)]
    pallas_call x0 -> x4, Pallas kernels: none -> 7.83 us  [the longest x1 3.12 us: sweeps(): pl.pallas_call(sweeps_kernel, out_shape=(jax.ShapeDtypeStruct((SUBLANES,...]
    all_to_all x2 -> x1, starting transfers between devices: 22.2 us -> 17.6 us  [body(): lax.all_to_all(packed.reshape(devices, packed.shape[0] // devices, LANES)...]
    unnamed x14 -> x8, local copies, waits for them, and re-layouts: 3.86 us -> 0.03 us
    convert_element_type x2 -> x0, local copies, waits for them, and re-layouts: 2.62 us -> none  [the longest x1 1.32 us: reweighted_solve(): quality = quality_block.astype(jnp.float32)]
    reduce_sum x1 -> x0, other arithmetic: 2.37 us -> none  [reweighted_solve(): jnp.sum(weight, axis=0)]
  transfers between devices with their start and end apart: 3 -> 2, of which waited for: 3 -> 2; matrix products, arithmetic and copies ran while one was open for 9% -> 0% of each run, Pallas kernels for 0% -> 3%
where the time goes in v2:
time: 62.9 us; the launch traced here: 62.7 us
  waiting for transfers between devices  34 us (54%)
  starting transfers between devices  19.5 us (31%)
  Pallas kernels  7.83 us (12%)
  between operations  0.72 us (1%)
    all_to_all x1, waiting for transfers between devices, body(): lax.all_to_all(packed.reshape(devices, packed.shape[0] // devices, LANES)...  28.1 us
    all_to_all x1, starting transfers between devices, body(): lax.all_to_all(packed.reshape(devices, packed.shape[0] // devices, LANES)...  17.6 us
    ppermute x1, waiting for transfers between devices, from_behind(): return lax.ppermute(block, axis, route)  5.88 us
    pallas_call x1, Pallas kernels, sweeps(): pl.pallas_call(sweeps_kernel, out_shape=(jax.ShapeDtypeStruct((SUBLANES,...  3.12 us
    pallas_call x1, Pallas kernels, pack(): pl.pallas_call(lambda *refs: pack_kernel(order, *refs), out_shape=jax.Sha...  2.82 us
    ppermute x1, starting transfers between devices, from_behind(): return lax.ppermute(block, axis, route)  1.93 us
    pallas_call x1, Pallas kernels, misfits(): pl.pallas_call(misfit_kernel, out_shape=jax.ShapeDtypeStruct((1, pixels),...  1.32 us
  transfers between devices with their start and end apart: 2, of which 2 were waited for; matrix products, arithmetic and copies ran while one was open for 0% of the time, Pallas kernels for 3%

profile of v2, /device:TPU:32, one launch (start us, length us, event | category | flops | bytes accessed | tf_op | source)
XLA Modules:
  0.0 62.7 jit_solution(1144823906052319765)
XLA Ops:
  0.6 2.8 %pack.1 = bf16[5120,128]{1,0:T(8,128)(2,1)} custom-call(bf16[5,128,512]{2,1,0:T(8,128)(2,1)} %refs_0_.1, bf16[5,128,512]{2,1,0:T(8,128)(2,1)} %refs_1_.1), custom_call_target="tpu_custom_call" | custom-call | tf_op jit(solution)/shard_map/pack/pallas_call | solution.py:87
  3.5 0.0 copy-start
  3.5 0.0 copy-start.1
  3.5 0.0 copy-start.2
  3.5 0.0 copy-start.3
  3.5 17.6 %all-to-all-start = ((bf16[128,40,128]{2,1,0:T(8,128)(2,1)}), bf16[128,40,128]{2,1,0:T(8,128)(2,1)S(1)}, u32[]{:S(2)}, u32[]{:S(2)}) async-start(bf16[128,40,128]{2,1,0:T(8,128)(2,1)} %bitcast.7), calls=%async_computation | async-start | bytes 2621440 | tf_op jit(solution)/shard_map/all_to_all | solution.py:247
  21.1 0.0 copy-done
  21.1 0.0 copy-done.1
  21.1 0.0 copy-done.2
  21.1 0.6 prepare.1
  21.7 28.1 %all-to-all-done = bf16[128,40,128]{2,1,0:T(8,128)(2,1)S(1)} async-done(((bf16[128,40,128]{2,1,0:T(8,128)(2,1)}), bf16[128,40,128]{2,1,0:T(8,128)(2,1)S(1)}, u32[]{:S(2)}, u32[]{:S(2)}) %all-to-all-start) | async-done | bytes 1310752 | tf_op jit(solution)/shard_map/all_to_all | solution.py:247
  49.9 0.0 copy-done.3
  49.9 3.1 %sweeps.1 = (f32[8,256]{1,0:T(8,128)S(1)}, f32[640,512]{1,0:T(8,128)S(1)}, f32[640,512]{1,0:T(8,128)S(1)}, bf16[512,512]{1,0:T(8,128)(2,1)S(1)}) custom-call(bf16[5120,128]{1,0:T(8,128)(2,1)S(1)} %bitcast.5, bf16[640,512]{1,0:T(8,128)(2,1)S(1)} %get-tuple-element.8.design_ref, bf16[160,640]{1,0:T(8,128)(2,1)S(1)} %get-tuple-element.9.spread_ref, ...), custom_call_target="tpu_custom_call" | custom-call | tf_op jit(solution)/shard_map/sweeps/pallas_call | solution.py:189
  53.0 1.9 %collective-permute-start = (f32[2,150]{1,0:T(2,128)S(1)}, f32[2,150]{1,0:T(2,128)S(1)}, u32[]{:S(2)}, u32[]{:S(2)}) collective-permute-start(f32[2,150]{1,0:T(2,128)S(1)} %slice.7), channel_id=1, source_target_pairs={{0,1},{1,2},{2,3},{3,4},{4,5},{5,6},{6,7},{7,8},{8,9},{9,10},{10,1... | collective-permute-start | bytes 3608 | tf_op jit(solution)/shard_map/ppermute | solution.py:34
  54.9 1.3 %misfit.1 = f32[1,512]{1,0:T(1,128)} custom-call(bf16[640,512]{1,0:T(8,128)(2,1)S(1)} %get-tuple-element.8.design_ref, f32[640,512]{1,0:T(8,128)S(1)} %get-tuple-element.10.phase_ref, f32[640,512]{1,0:T(8,128)S(1)} %get-tuple-element.11.quality_ref, bf16[512,512]{1,0:T(8,128)(2,1)S(1)} %get-tuple-element.12.parts_ref), custom_call_target="tpu_custom_call" | custom-call | tf_op jit(solution)/shard_map/misfit/pallas_call | solution.py:232
  56.2 5.9 %collective-permute-done = f32[2,150]{1,0:T(2,128)S(1)} collective-permute-done((f32[2,150]{1,0:T(2,128)S(1)}, f32[2,150]{1,0:T(2,128)S(1)}, u32[]{:S(2)}, u32[]{:S(2)}) %collective-permute-start) | collective-permute-done | bytes 1232 | tf_op jit(solution)/shard_map/ppermute | solution.py:34
  62.1 0.6 add_bitcast_fusion
  (1 shorter events, 0.0 us)
Async XLA Ops:
  3.5 17.6 %copy-start = (bf16[150,640]{1,0:T(8,128)(2,1)S(1)}, bf16[150,640]{1,0:T(8,128)(2,1)}, u32[]{:S(2)}) copy-start(bf16[150,640]{1,0:T(8,128)(2,1)} %inverse_ref.1) | copy-start | bytes 576004
  3.5 17.6 %copy-start.1 = (s32[640,2]{0,1:T(2,128)S(1)}, s32[640,2]{0,1:T(2,128)}, u32[]{:S(2)}) copy-start(s32[640,2]{0,1:T(2,128)} %param.8) | copy-start | bytes 15364
  3.5 17.6 %copy-start.2 = (s32[1,640]{1,0:T(1,128)S(1)}, s32[1,640]{1,0:T(1,128)}, u32[]{:S(2)}) copy-start(s32[1,640]{1,0:T(1,128)} %constant.2.clone.arrival_ref) | copy-start | bytes 7684
  3.5 46.4 %copy-start.3 = (s32[1,512]{1,0:T(1,128)S(1)}, s32[1,512]{1,0:T(1,128)}, u32[]{:S(2)}) copy-start(s32[1,512]{1,0:T(1,128)} %footprint_ref.1) | copy-start | bytes 6148
  3.5 46.3 %all-to-all-start = ((bf16[128,40,128]{2,1,0:T(8,128)(2,1)}), bf16[128,40,128]{2,1,0:T(8,128)(2,1)S(1)}, u32[]{:S(2)}, u32[]{:S(2)}) async-start(bf16[128,40,128]{2,1,0:T(8,128)(2,1)} %bitcast.7), calls=%async_computation | async-start | bytes 2621440 | tf_op jit(solution)/shard_map/all_to_all | solution.py:247
  53.0 9.1 %collective-permute-start = (f32[2,150]{1,0:T(2,128)S(1)}, f32[2,150]{1,0:T(2,128)S(1)}, u32[]{:S(2)}, u32[]{:S(2)}) collective-permute-start(f32[2,150]{1,0:T(2,128)S(1)} %slice.7), channel_id=1, source_target_pairs={{0,1},{1,2},{2,3},{3,4},{4,5},{5,6},{6,7},{7,8},{8,9},{9,10},{10,1... | collective-permute-start | bytes 3608 | tf_op jit(solution)/shard_map/ppermute | solution.py:34

commit v3 on v2

--- a/solution.py
+++ b/solution.py
@@ -14,7 +14,7 @@
 EPOCH_ROWS = 160
 EPOCH_DEPTH = 256
 HALF = 256
-ORDER_SEED = 102
+ORDER_SEED = 121
 
 phase_scale = 1.5
 scale_squared = phase_scale**2
@@ -43,22 +43,52 @@
     return jnp.where(hit, value, 0.0).astype(jnp.bfloat16)
 
 
-def pack_kernel(order, phase_hbm, quality_hbm, packed_ref, phase_ref, quality_ref, sems):
+def reorder_pairs(arrival_ref, named_ref, inverse_ref, design_ref, spread_ref):
+    pairs = named_ref.shape[1]
+    reorder = (lax.broadcasted_iota(jnp.int32, (pairs, pairs), 0) == arrival_ref[...]).astype(jnp.bfloat16)
+    named = jnp.dot(
+        named_ref[...].astype(jnp.float32).astype(jnp.bfloat16), reorder, preferred_element_type=jnp.float32
+    )
+    epochs = lax.broadcasted_iota(jnp.int32, (EPOCH_DEPTH, pairs), 0).astype(jnp.float32)
+    later = (epochs == named[1:2, :]).astype(jnp.float32)
+    earlier = (epochs == named[0:1, :]).astype(jnp.float32)
+    design = (later - earlier).T.astype(jnp.bfloat16)
+    design_ref[:, 0:EPOCH_DEPTH] = design
+    design_ref[:, EPOCH_DEPTH:] = design
+    spread = jnp.dot(inverse_ref[...], reorder, preferred_element_type=jnp.float32).astype(jnp.bfloat16)
+    spread_ref[...] = jnp.zeros_like(spread_ref)
+    spread_ref[0 : inverse_ref.shape[0], :] = spread
+
+
+def pack_kernel(
+    order, phase_hbm, quality_hbm, arrival_hbm, named_hbm, inverse_hbm, packed_ref, design_ref, spread_ref,
+    phase_ref, quality_ref, arrival_ref, named_ref, inverse_ref, small_sems, sems,
+):
     pairs, slabs, pixels = phase_ref.shape
     step = slabs // sems.shape[0]
-    copies = []
+    small = [
+        pltpu.make_async_copy(source, target, small_sems.at[at])
+        for at, (source, target) in enumerate(
+            ((arrival_hbm, arrival_ref), (named_hbm, named_ref), (inverse_hbm, inverse_ref))
+        )
+    ]
+    large = []
     for part in range(sems.shape[0]):
         for which, (source, target) in enumerate(((phase_hbm, phase_ref), (quality_hbm, quality_ref))):
             span = pl.ds(part * step, step)
-            copies.append(
+            large.append(
                 pltpu.make_async_copy(source.at[:, span, :], target.at[:, span, :], sems.at[part, which])
             )
-            copies[-1].start()
+    for copy in small + large:
+        copy.start()
+    for copy in small:
+        copy.wait()
+    reorder_pairs(arrival_ref, named_ref, inverse_ref, design_ref, spread_ref)
     place = {slab: at for at, slab in enumerate(order)}
     swap = swap_rows(GROUP, 1.0)
     for group in range(slabs // GROUP):
         if group * GROUP % step == 0:
-            for copy in copies[2 * (group * GROUP // step) :][:2]:
+            for copy in large[2 * (group * GROUP // step) :][:2]:
                 copy.wait()
         rows = [
             jnp.concatenate(
@@ -81,54 +111,25 @@
                 ).astype(jnp.bfloat16)
 
 
-def pack(interferograms, coherence, order):
+def pack(interferograms, coherence, pair_epochs, inverse, order):
     pairs, slabs, pixels = interferograms.shape
     rows = slabs * pairs * 2 * pixels // LANES
+    arrival = np.array([[device * pairs + k for device in order for k in range(pairs)]], np.int32)
+    taken = (interferograms, coherence, jnp.asarray(arrival), pair_epochs.T, inverse)
     return pl.pallas_call(
         lambda *refs: pack_kernel(order, *refs),
-        out_shape=jax.ShapeDtypeStruct((rows, LANES), jnp.bfloat16),
-        in_specs=[HBM] * 2,
-        out_specs=VMEM,
-        scratch_shapes=[
-            pltpu.VMEM(interferograms.shape, jnp.bfloat16),
-            pltpu.VMEM(coherence.shape, jnp.bfloat16),
-            pltpu.SemaphoreType.DMA((2, 2)),
-        ],
-        compiler_params=pltpu.CompilerParams(vmem_limit_bytes=60 << 20),
+        out_shape=(
+            jax.ShapeDtypeStruct((rows, LANES), jnp.bfloat16),
+            jax.ShapeDtypeStruct((arrival.shape[1], 2 * EPOCH_DEPTH), jnp.bfloat16),
+            jax.ShapeDtypeStruct((EPOCH_ROWS, arrival.shape[1]), jnp.bfloat16),
+        ),
+        in_specs=[HBM] * len(taken),
+        out_specs=[VMEM] * 3,
+        scratch_shapes=[pltpu.VMEM(array.shape, array.dtype) for array in taken]
+        + [pltpu.SemaphoreType.DMA((3,)), pltpu.SemaphoreType.DMA((2, 2))],
+        compiler_params=pltpu.CompilerParams(vmem_limit_bytes=24 << 20),
         name="pack",
-    )(interferograms, coherence)
-
-
-def prepare_kernel(arrival_ref, named_ref, inverse_ref, design_ref, spread_ref):
-    pairs = named_ref.shape[1]
-    reorder = (lax.broadcasted_iota(jnp.int32, (pairs, pairs), 0) == arrival_ref[...]).astype(jnp.bfloat16)
-    named = jnp.dot(
-        named_ref[...].astype(jnp.float32).astype(jnp.bfloat16), reorder, preferred_element_type=jnp.float32
-    )
-    epochs = lax.broadcasted_iota(jnp.int32, (EPOCH_DEPTH, pairs), 0).astype(jnp.float32)
-    later = (epochs == named[1:2, :]).astype(jnp.float32)
-    earlier = (epochs == named[0:1, :]).astype(jnp.float32)
-    design = (later - earlier).T.astype(jnp.bfloat16)
-    design_ref[:, 0:EPOCH_DEPTH] = design
-    design_ref[:, EPOCH_DEPTH:] = design
-    spread = jnp.dot(inverse_ref[...], reorder, preferred_element_type=jnp.float32).astype(jnp.bfloat16)
-    spread_ref[...] = jnp.zeros_like(spread_ref)
-    spread_ref[0 : inverse_ref.shape[0], :] = spread
-
-
-def prepare(pair_epochs, inverse, arrival):
-    pairs = pair_epochs.shape[0]
-    return pl.pallas_call(
-        prepare_kernel,
-        out_shape=(
-            jax.ShapeDtypeStruct((pairs, 2 * EPOCH_DEPTH), jnp.bfloat16),
-            jax.ShapeDtypeStruct((EPOCH_ROWS, pairs), jnp.bfloat16),
-        ),
-        in_specs=[VMEM] * 3,
-        out_specs=[VMEM] * 2,
-        compiler_params=pltpu.CompilerParams(vmem_limit_bytes=16 << 20),
-        name="prepare",
-    )(arrival, pair_epochs.T, inverse)
+    )(*(pltpu.with_memory_space_constraint(array, pltpu.HBM) for array in taken))
 
 
 def sweeps_kernel(
@@ -243,7 +244,7 @@
 def body(interferograms, coherence, pair_epochs, inverse, footprint):
     devices = lax.axis_size("pair")
     order = exchange_order(devices)
-    packed = pack(interferograms, coherence, order)
+    packed, design, spread = pack(interferograms, coherence, pair_epochs, inverse, order)
     blocks = lax.all_to_all(
         packed.reshape(devices, packed.shape[0] // devices, LANES),
         "pair",
@@ -252,9 +253,6 @@
         tiled=True,
         axis_index_groups=[order],
     )
-    local = interferograms.shape[0]
-    arrival = np.array([[device * local + k for device in order for k in range(local)]], np.int32)
-    design, spread = prepare(pair_epochs, inverse, jnp.asarray(arrival))
     cells, phase, quality, parts = sweeps(blocks.reshape(packed.shape), design, spread, footprint)
     cells_tile = footprint.shape[1] // PPC
     epochs = inverse.shape[0]

time: 62.9 us -> 61 us (0.970)
  blocking collectives: 0 us -> 44.9 us
  waiting for transfers between devices: 34 us -> 5.88 us
  starting transfers between devices: 19.5 us -> 1.93 us
  Pallas kernels: 7.83 us -> 6.93 us
    all_to_all x0 -> x1, blocking collectives: none -> 44.9 us  [body(): lax.all_to_all(packed.reshape(devices, packed.shape[0] // devices, LANES)...]
    all_to_all x1 -> x0, waiting for transfers between devices: 28.1 us -> none  [body(): lax.all_to_all(packed.reshape(devices, packed.shape[0] // devices, LANES)...]
    all_to_all x1 -> x0, starting transfers between devices: 17.6 us -> none  [body(): lax.all_to_all(packed.reshape(devices, packed.shape[0] // devices, LANES)...]
    pallas_call x2 -> x1, Pallas kernels: 3.4 us -> 2.57 us  [pack(): pl.pallas_call(lambda *refs: pack_kernel(order, *refs), out_shape=(jax.Sh...]
  transfers between devices with their start and end apart: 2 -> 1, of which waited for: 2 -> 1; matrix products, arithmetic and copies ran while one was open for 0% -> 0% of each run, Pallas kernels for 3% -> 2%
where the time goes in v3:
time: 61 us; the launch traced here: 60.9 us
  blocking collectives  44.9 us (74%)
  Pallas kernels  6.93 us (11%)
  waiting for transfers between devices  5.88 us (10%)
  starting transfers between devices  1.93 us (3%)
  between operations  0.66 us (1%)
    all_to_all x1, blocking collectives, body(): lax.all_to_all(packed.reshape(devices, packed.shape[0] // devices, LANES)...  44.9 us
    ppermute x1, waiting for transfers between devices, from_behind(): return lax.ppermute(block, axis, route)  5.88 us
    pallas_call x1, Pallas kernels, sweeps(): pl.pallas_call(sweeps_kernel, out_shape=(jax.ShapeDtypeStruct((SUBLANES,...  3.05 us
    pallas_call x1, Pallas kernels, pack(): pl.pallas_call(lambda *refs: pack_kernel(order, *refs), out_shape=(jax.Sh...  2.57 us
    ppermute x1, starting transfers between devices, from_behind(): return lax.ppermute(block, axis, route)  1.93 us
    pallas_call x1, Pallas kernels, misfits(): pl.pallas_call(misfit_kernel, out_shape=jax.ShapeDtypeStruct((1, pixels),...  1.31 us
  transfers between devices with their start and end apart: 1, of which 1 were waited for; matrix products, arithmetic and copies ran while one was open for 0% of the time, Pallas kernels for 2%

profile of v3, /device:TPU:32, one launch (start us, length us, event | category | flops | bytes accessed | tf_op | source)
XLA Modules:
  0.0 60.9 jit_solution(6580231876619079435)
XLA Ops:
  0.6 2.6 %pack.1 = (bf16[5120,128]{1,0:T(8,128)(2,1)S(1)}, bf16[640,512]{1,0:T(8,128)(2,1)S(1)}, bf16[160,640]{1,0:T(8,128)(2,1)S(1)}) custom-call(bf16[5,128,512]{2,1,0:T(8,128)(2,1)} %refs_0_.1, bf16[5,128,512]{2,1,0:T(8,128)(2,1)} %refs_1_.1, s32[1,640]{1,0:T(1,128)} %constant.2.clone.refs_2_, s32[2,640]{1,0:T(2,128)} %bitcast.7, bf16[150,640]{1,0:T(8,128)(2,1)} %refs_4_.1), custom_call_target="tpu_custom_call" | custom-call | tf_op jit(solution)/shard_map/pack/pallas_call | solution.py:119
  3.2 0.0 copy-start
  3.2 44.9 %all_to_all.5 = bf16[128,40,128]{2,1,0:T(8,128)(2,1)S(1)} all-to-all(bf16[128,40,128]{2,1,0:T(8,128)(2,1)S(1)} %bitcast.6), channel_id=1, replica_groups={{212,214,20,22,68,70,100,102,192,194,60,62,148,150,244,246,116,118,24,2..., dimensions={0} | all-to-all | bytes 2621440 | tf_op jit(solution)/shard_map/all_to_all | solution.py:248
  48.1 0.0 copy-done
  48.1 3.0 %sweeps.1 = (f32[8,256]{1,0:T(8,128)S(1)}, f32[640,512]{1,0:T(8,128)S(1)}, f32[640,512]{1,0:T(8,128)S(1)}, bf16[512,512]{1,0:T(8,128)(2,1)S(1)}) custom-call(bf16[5120,128]{1,0:T(8,128)(2,1)S(1)} %bitcast.5, bf16[640,512]{1,0:T(8,128)(2,1)S(1)} %get-tuple-element.9.design_ref, bf16[160,640]{1,0:T(8,128)(2,1)S(1)} %get-tuple-element.11.spread_ref, ...), custom_call_target="tpu_custom_call" | custom-call | tf_op jit(solution)/shard_map/sweeps/pallas_call | solution.py:190
  51.1 1.9 %collective-permute-start = (f32[2,150]{1,0:T(2,128)S(1)}, f32[2,150]{1,0:T(2,128)S(1)}, u32[]{:S(2)}, u32[]{:S(2)}) collective-permute-start(f32[2,150]{1,0:T(2,128)S(1)} %slice.7), channel_id=1, source_target_pairs={{0,1},{1,2},{2,3},{3,4},{4,5},{5,6},{6,7},{7,8},{8,9},{9,10},{10,1... | collective-permute-start | bytes 3608 | tf_op jit(solution)/shard_map/ppermute | solution.py:34
  53.1 1.3 %misfit.1 = f32[1,512]{1,0:T(1,128)} custom-call(bf16[640,512]{1,0:T(8,128)(2,1)S(1)} %get-tuple-element.9.design_ref, f32[640,512]{1,0:T(8,128)S(1)} %get-tuple-element.12.phase_ref, f32[640,512]{1,0:T(8,128)S(1)} %get-tuple-element.13.quality_ref, bf16[512,512]{1,0:T(8,128)(2,1)S(1)} %get-tuple-element.14.parts_ref), custom_call_target="tpu_custom_call" | custom-call | tf_op jit(solution)/shard_map/misfit/pallas_call | solution.py:233
  54.4 5.9 %collective-permute-done = f32[2,150]{1,0:T(2,128)S(1)} collective-permute-done((f32[2,150]{1,0:T(2,128)S(1)}, f32[2,150]{1,0:T(2,128)S(1)}, u32[]{:S(2)}, u32[]{:S(2)}) %collective-permute-start) | collective-permute-done | bytes 1232 | tf_op jit(solution)/shard_map/ppermute | solution.py:34
  60.3 0.6 add_bitcast_fusion
  (1 shorter events, 0.0 us)
Async XLA Ops:
  3.2 44.9 %copy-start = (s32[1,512]{1,0:T(1,128)S(1)}, s32[1,512]{1,0:T(1,128)}, u32[]{:S(2)}) copy-start(s32[1,512]{1,0:T(1,128)} %footprint_ref.1) | copy-start | bytes 6148
  51.1 9.1 %collective-permute-start = (f32[2,150]{1,0:T(2,128)S(1)}, f32[2,150]{1,0:T(2,128)S(1)}, u32[]{:S(2)}, u32[]{:S(2)}) collective-permute-start(f32[2,150]{1,0:T(2,128)S(1)} %slice.7), channel_id=1, source_target_pairs={{0,1},{1,2},{2,3},{3,4},{4,5},{5,6},{6,7},{7,8},{8,9},{9,10},{10,1... | collective-permute-start | bytes 3608 | tf_op jit(solution)/shard_map/ppermute | solution.py:34

commit v4 on v3

--- a/solution.py
+++ b/solution.py
@@ -126,7 +126,7 @@
         in_specs=[HBM] * len(taken),
         out_specs=[VMEM] * 3,
         scratch_shapes=[pltpu.VMEM(array.shape, array.dtype) for array in taken]
-        + [pltpu.SemaphoreType.DMA((3,)), pltpu.SemaphoreType.DMA((2, 2))],
+        + [pltpu.SemaphoreType.DMA((3,)), pltpu.SemaphoreType.DMA((1, 2))],
         compiler_params=pltpu.CompilerParams(vmem_limit_bytes=24 << 20),
         name="pack",
     )(*(pltpu.with_memory_space_constraint(array, pltpu.HBM) for array in taken))

time: 61 us -> 60.7 us (level)
  no operation moved by 1% of the time
where the time goes in v4:
time: 60.7 us; the launch traced here: 60.6 us
  blocking collectives  44.9 us (74%)
  Pallas kernels  6.65 us (11%)
  waiting for transfers between devices  5.89 us (10%)
  starting transfers between devices  1.93 us (3%)
  between operations  0.66 us (1%)
    all_to_all x1, blocking collectives, body(): lax.all_to_all(packed.reshape(devices, packed.shape[0] // devices, LANES)...  44.9 us
    ppermute x1, waiting for transfers between devices, from_behind(): return lax.ppermute(block, axis, route)  5.89 us
    pallas_call x1, Pallas kernels, sweeps(): pl.pallas_call(sweeps_kernel, out_shape=(jax.ShapeDtypeStruct((SUBLANES,...  3.05 us
    pallas_call x1, Pallas kernels, pack(): pl.pallas_call(lambda *refs: pack_kernel(order, *refs), out_shape=(jax.Sh...  2.29 us
    ppermute x1, starting transfers between devices, from_behind(): return lax.ppermute(block, axis, route)  1.93 us
    pallas_call x1, Pallas kernels, misfits(): pl.pallas_call(misfit_kernel, out_shape=jax.ShapeDtypeStruct((1, pixels),...  1.3 us
  transfers between devices with their start and end apart: 1, of which 1 were waited for; matrix products, arithmetic and copies ran while one was open for 0% of the time, Pallas kernels for 2%

profile of v4, /device:TPU:32, one launch (start us, length us, event | category | flops | bytes accessed | tf_op | source)
XLA Modules:
  0.0 60.6 jit_solution(951608255460521270)
XLA Ops:
  0.6 2.3 %pack.1 = (bf16[5120,128]{1,0:T(8,128)(2,1)S(1)}, bf16[640,512]{1,0:T(8,128)(2,1)S(1)}, bf16[160,640]{1,0:T(8,128)(2,1)S(1)}) custom-call(bf16[5,128,512]{2,1,0:T(8,128)(2,1)} %refs_0_.1, bf16[5,128,512]{2,1,0:T(8,128)(2,1)} %refs_1_.1, s32[1,640]{1,0:T(1,128)} %constant.2.clone.refs_2_, s32[2,640]{1,0:T(2,128)} %bitcast.7, bf16[150,640]{1,0:T(8,128)(2,1)} %refs_4_.1), custom_call_target="tpu_custom_call" | custom-call | tf_op jit(solution)/shard_map/pack/pallas_call | solution.py:119
  2.9 0.0 copy-start
  2.9 44.9 %all_to_all.5 = bf16[128,40,128]{2,1,0:T(8,128)(2,1)S(1)} all-to-all(bf16[128,40,128]{2,1,0:T(8,128)(2,1)S(1)} %bitcast.6), channel_id=1, replica_groups={{212,214,20,22,68,70,100,102,192,194,60,62,148,150,244,246,116,118,24,2..., dimensions={0} | all-to-all | bytes 2621440 | tf_op jit(solution)/shard_map/all_to_all | solution.py:248
  47.8 0.0 copy-done
  47.8 3.0 %sweeps.1 = (f32[8,256]{1,0:T(8,128)S(1)}, f32[640,512]{1,0:T(8,128)S(1)}, f32[640,512]{1,0:T(8,128)S(1)}, bf16[512,512]{1,0:T(8,128)(2,1)S(1)}) custom-call(bf16[5120,128]{1,0:T(8,128)(2,1)S(1)} %bitcast.5, bf16[640,512]{1,0:T(8,128)(2,1)S(1)} %get-tuple-element.9.design_ref, bf16[160,640]{1,0:T(8,128)(2,1)S(1)} %get-tuple-element.11.spread_ref, ...), custom_call_target="tpu_custom_call" | custom-call | tf_op jit(solution)/shard_map/sweeps/pallas_call | solution.py:190
  50.9 1.9 %collective-permute-start = (f32[2,150]{1,0:T(2,128)S(1)}, f32[2,150]{1,0:T(2,128)S(1)}, u32[]{:S(2)}, u32[]{:S(2)}) collective-permute-start(f32[2,150]{1,0:T(2,128)S(1)} %slice.7), channel_id=1, source_target_pairs={{0,1},{1,2},{2,3},{3,4},{4,5},{5,6},{6,7},{7,8},{8,9},{9,10},{10,1... | collective-permute-start | bytes 3608 | tf_op jit(solution)/shard_map/ppermute | solution.py:34
  52.8 1.3 %misfit.1 = f32[1,512]{1,0:T(1,128)} custom-call(bf16[640,512]{1,0:T(8,128)(2,1)S(1)} %get-tuple-element.9.design_ref, f32[640,512]{1,0:T(8,128)S(1)} %get-tuple-element.12.phase_ref, f32[640,512]{1,0:T(8,128)S(1)} %get-tuple-element.13.quality_ref, bf16[512,512]{1,0:T(8,128)(2,1)S(1)} %get-tuple-element.14.parts_ref), custom_call_target="tpu_custom_call" | custom-call | tf_op jit(solution)/shard_map/misfit/pallas_call | solution.py:233
  54.1 5.9 %collective-permute-done = f32[2,150]{1,0:T(2,128)S(1)} collective-permute-done((f32[2,150]{1,0:T(2,128)S(1)}, f32[2,150]{1,0:T(2,128)S(1)}, u32[]{:S(2)}, u32[]{:S(2)}) %collective-permute-start) | collective-permute-done | bytes 1232 | tf_op jit(solution)/shard_map/ppermute | solution.py:34
  60.0 0.6 add_bitcast_fusion
  (1 shorter events, 0.0 us)
Async XLA Ops:
  2.9 44.9 %copy-start = (s32[1,512]{1,0:T(1,128)S(1)}, s32[1,512]{1,0:T(1,128)}, u32[]{:S(2)}) copy-start(s32[1,512]{1,0:T(1,128)} %footprint_ref.1) | copy-start | bytes 6148
  50.9 9.1 %collective-permute-start = (f32[2,150]{1,0:T(2,128)S(1)}, f32[2,150]{1,0:T(2,128)S(1)}, u32[]{:S(2)}, u32[]{:S(2)}) collective-permute-start(f32[2,150]{1,0:T(2,128)S(1)} %slice.7), channel_id=1, source_target_pairs={{0,1},{1,2},{2,3},{3,4},{4,5},{5,6},{6,7},{7,8},{8,9},{9,10},{10,1... | collective-permute-start | bytes 3608 | tf_op jit(solution)/shard_map/ppermute | solution.py:34

commit v5 on v4

--- a/solution.py
+++ b/solution.py
@@ -43,7 +43,7 @@
     return jnp.where(hit, value, 0.0).astype(jnp.bfloat16)
 
 
-def reorder_pairs(arrival_ref, named_ref, inverse_ref, design_ref, spread_ref):
+def reorder_pairs(arrival_ref, named_ref, design_ref, reorder_ref):
     pairs = named_ref.shape[1]
     reorder = (lax.broadcasted_iota(jnp.int32, (pairs, pairs), 0) == arrival_ref[...]).astype(jnp.bfloat16)
     named = jnp.dot(
@@ -55,21 +55,19 @@
     design = (later - earlier).T.astype(jnp.bfloat16)
     design_ref[:, 0:EPOCH_DEPTH] = design
     design_ref[:, EPOCH_DEPTH:] = design
-    spread = jnp.dot(inverse_ref[...], reorder, preferred_element_type=jnp.float32).astype(jnp.bfloat16)
-    spread_ref[...] = jnp.zeros_like(spread_ref)
-    spread_ref[0 : inverse_ref.shape[0], :] = spread
+    reorder_ref[...] = reorder
 
 
 def pack_kernel(
-    order, phase_hbm, quality_hbm, arrival_hbm, named_hbm, inverse_hbm, packed_ref, design_ref, spread_ref,
-    phase_ref, quality_ref, arrival_ref, named_ref, inverse_ref, small_sems, sems,
+    order, phase_hbm, quality_hbm, arrival_hbm, named_hbm, packed_ref, design_ref, reorder_ref,
+    phase_ref, quality_ref, arrival_ref, named_ref, small_sems, sems,
 ):
     pairs, slabs, pixels = phase_ref.shape
     step = slabs // sems.shape[0]
     small = [
         pltpu.make_async_copy(source, target, small_sems.at[at])
         for at, (source, target) in enumerate(
-            ((arrival_hbm, arrival_ref), (named_hbm, named_ref), (inverse_hbm, inverse_ref))
+            ((arrival_hbm, arrival_ref), (named_hbm, named_ref))
         )
     ]
     large = []
@@ -83,7 +81,7 @@
         copy.start()
     for copy in small:
         copy.wait()
-    reorder_pairs(arrival_ref, named_ref, inverse_ref, design_ref, spread_ref)
+    reorder_pairs(arrival_ref, named_ref, design_ref, reorder_ref)
     place = {slab: at for at, slab in enumerate(order)}
     swap = swap_rows(GROUP, 1.0)
     for group in range(slabs // GROUP):
@@ -111,30 +109,30 @@
                 ).astype(jnp.bfloat16)
 
 
-def pack(interferograms, coherence, pair_epochs, inverse, order):
+def pack(interferograms, coherence, pair_epochs, order):
     pairs, slabs, pixels = interferograms.shape
     rows = slabs * pairs * 2 * pixels // LANES
     arrival = np.array([[device * pairs + k for device in order for k in range(pairs)]], np.int32)
-    taken = (interferograms, coherence, jnp.asarray(arrival), pair_epochs.T, inverse)
+    taken = (interferograms, coherence, jnp.asarray(arrival), pair_epochs.T)
     return pl.pallas_call(
         lambda *refs: pack_kernel(order, *refs),
         out_shape=(
             jax.ShapeDtypeStruct((rows, LANES), jnp.bfloat16),
             jax.ShapeDtypeStruct((arrival.shape[1], 2 * EPOCH_DEPTH), jnp.bfloat16),
-            jax.ShapeDtypeStruct((EPOCH_ROWS, arrival.shape[1]), jnp.bfloat16),
+            jax.ShapeDtypeStruct((arrival.shape[1], arrival.shape[1]), jnp.bfloat16),
         ),
         in_specs=[HBM] * len(taken),
         out_specs=[VMEM] * 3,
         scratch_shapes=[pltpu.VMEM(array.shape, array.dtype) for array in taken]
-        + [pltpu.SemaphoreType.DMA((3,)), pltpu.SemaphoreType.DMA((1, 2))],
+        + [pltpu.SemaphoreType.DMA((2,)), pltpu.SemaphoreType.DMA((1, 2))],
         compiler_params=pltpu.CompilerParams(vmem_limit_bytes=24 << 20),
         name="pack",
     )(*(pltpu.with_memory_space_constraint(array, pltpu.HBM) for array in taken))
 
 
 def sweeps_kernel(
-    received_ref, design_ref, spread_ref, footprint_ref, cells_ref, phase_ref, quality_ref, parts_ref,
-    motion_ref, weighted_ref, modeled_ref,
+    received_ref, design_ref, reorder_ref, inverse_ref, footprint_ref, cells_ref, phase_ref, quality_ref, parts_ref,
+    spread_ref, motion_ref, weighted_ref, modeled_ref,
 ):
     pairs, pixels = phase_ref.shape
     chunks = pixels // LANES
@@ -154,6 +152,10 @@
                     jnp.bfloat16
                 )
     parts_ref[...] = jnp.zeros_like(parts_ref)
+    spread_ref[...] = jnp.zeros_like(spread_ref)
+    spread_ref[0 : inverse_ref.shape[0], :] = jnp.dot(
+        inverse_ref[...], reorder_ref[...], preferred_element_type=jnp.float32
+    ).astype(jnp.bfloat16)
     for repeat in range(ITERS):
         for half in range(0, pixels, HALF):
             columns = pl.ds(half, HALF)
@@ -184,7 +186,7 @@
     )
 
 
-def sweeps(received, design, spread, footprint):
+def sweeps(received, design, reorder, inverse, footprint):
     pairs = design.shape[0]
     pixels = footprint.shape[1]
     return pl.pallas_call(
@@ -195,16 +197,17 @@
             jax.ShapeDtypeStruct((pairs, pixels), jnp.float32),
             jax.ShapeDtypeStruct((2 * EPOCH_DEPTH, pixels), jnp.bfloat16),
         ),
-        in_specs=[VMEM] * 4,
+        in_specs=[VMEM] * 5,
         out_specs=[VMEM] * 4,
         scratch_shapes=[
+            pltpu.VMEM((EPOCH_ROWS, pairs), jnp.bfloat16),
             pltpu.VMEM((EPOCH_ROWS, pixels), jnp.float32),
             pltpu.VMEM((pairs, pixels), jnp.bfloat16),
             pltpu.VMEM((pairs, pixels), jnp.float32),
         ],
         compiler_params=pltpu.CompilerParams(vmem_limit_bytes=24 << 20),
         name="sweeps",
-    )(received, design, spread, footprint)
+    )(received, design, reorder, inverse, footprint)
 
 
 def misfit_kernel(design_ref, phase_ref, quality_ref, parts_ref, misfit_ref, modeled_ref):
@@ -244,7 +247,7 @@
 def body(interferograms, coherence, pair_epochs, inverse, footprint):
     devices = lax.axis_size("pair")
     order = exchange_order(devices)
-    packed, design, spread = pack(interferograms, coherence, pair_epochs, inverse, order)
+    packed, design, reorder = pack(interferograms, coherence, pair_epochs, order)
     blocks = lax.all_to_all(
         packed.reshape(devices, packed.shape[0] // devices, LANES),
         "pair",
@@ -253,7 +256,7 @@
         tiled=True,
         axis_index_groups=[order],
     )
-    cells, phase, quality, parts = sweeps(blocks.reshape(packed.shape), design, spread, footprint)
+    cells, phase, quality, parts = sweeps(blocks.reshape(packed.shape), design, reorder, inverse, footprint)
     cells_tile = footprint.shape[1] // PPC
     epochs = inverse.shape[0]
     own_cells = cells[:cells_tile, :epochs]

time: 60.7 us -> 60.8 us (level)
  no operation moved by 1% of the time
where the time goes in v5:
time: 60.8 us; the launch traced here: 60.6 us
  blocking collectives  45 us (74%)
  Pallas kernels  6.56 us (11%)
  waiting for transfers between devices  5.88 us (10%)
  starting transfers between devices  1.93 us (3%)
  between operations  0.67 us (1%)
    all_to_all x1, blocking collectives, body(): lax.all_to_all(packed.reshape(devices, packed.shape[0] // devices, LANES)...  45 us
    ppermute x1, waiting for transfers between devices, from_behind(): return lax.ppermute(block, axis, route)  5.88 us
    pallas_call x1, Pallas kernels, sweeps(): pl.pallas_call(sweeps_kernel, out_shape=(jax.ShapeDtypeStruct((SUBLANES,...  3.34 us
    ppermute x1, starting transfers between devices, from_behind(): return lax.ppermute(block, axis, route)  1.93 us
    pallas_call x1, Pallas kernels, pack(): pl.pallas_call(lambda *refs: pack_kernel(order, *refs), out_shape=(jax.Sh...  1.9 us
    pallas_call x1, Pallas kernels, misfits(): pl.pallas_call(misfit_kernel, out_shape=jax.ShapeDtypeStruct((1, pixels),...  1.31 us
  transfers between devices with their start and end apart: 1, of which 1 were waited for; matrix products, arithmetic and copies ran while one was open for 0% of the time, Pallas kernels for 2%

profile of v5, /device:TPU:32, one launch (start us, length us, event | category | flops | bytes accessed | tf_op | source)
XLA Modules:
  0.0 60.6 jit_solution(11406741854721204884)
XLA Ops:
  0.6 1.9 %pack.1 = (bf16[5120,128]{1,0:T(8,128)(2,1)S(1)}, bf16[640,512]{1,0:T(8,128)(2,1)S(1)}, bf16[640,640]{1,0:T(8,128)(2,1)S(1)}) custom-call(bf16[5,128,512]{2,1,0:T(8,128)(2,1)} %refs_0_.1, bf16[5,128,512]{2,1,0:T(8,128)(2,1)} %refs_1_.1, s32[1,640]{1,0:T(1,128)} %constant.2.clone.refs_2_, s32[2,640]{1,0:T(2,128)} %bitcast.7), custom_call_target="tpu_custom_call" | custom-call | tf_op jit(solution)/shard_map/pack/pallas_call | solution.py:117
  2.5 0.0 copy-start
  2.6 0.0 copy-start.1
  2.6 45.0 %all_to_all.5 = bf16[128,40,128]{2,1,0:T(8,128)(2,1)S(1)} all-to-all(bf16[128,40,128]{2,1,0:T(8,128)(2,1)S(1)} %bitcast.6), channel_id=1, replica_groups={{212,214,20,22,68,70,100,102,192,194,60,62,148,150,244,246,116,118,24,2..., dimensions={0} | all-to-all | bytes 2621440 | tf_op jit(solution)/shard_map/all_to_all | solution.py:251
  47.6 0.0 copy-done
  47.6 0.0 copy-done.1
  47.6 3.3 %sweeps.1 = (f32[8,256]{1,0:T(8,128)S(1)}, f32[640,512]{1,0:T(8,128)S(1)}, f32[640,512]{1,0:T(8,128)S(1)}, bf16[512,512]{1,0:T(8,128)(2,1)S(1)}) custom-call(bf16[5120,128]{1,0:T(8,128)(2,1)S(1)} %bitcast.5, bf16[640,512]{1,0:T(8,128)(2,1)S(1)} %get-tuple-element.9.design_ref, bf16[640,640]{1,0:T(8,128)(2,1)S(1)} %get-tuple-element.11.reorder_ref, ...), custom_call_target="tpu_custom_call" | custom-call | tf_op jit(solution)/shard_map/sweeps/pallas_call | solution.py:192
  50.9 1.9 %collective-permute-start = (f32[2,150]{1,0:T(2,128)S(1)}, f32[2,150]{1,0:T(2,128)S(1)}, u32[]{:S(2)}, u32[]{:S(2)}) collective-permute-start(f32[2,150]{1,0:T(2,128)S(1)} %slice.7), channel_id=1, source_target_pairs={{0,1},{1,2},{2,3},{3,4},{4,5},{5,6},{6,7},{7,8},{8,9},{9,10},{10,1... | collective-permute-start | bytes 3608 | tf_op jit(solution)/shard_map/ppermute | solution.py:34
  52.9 1.3 %misfit.1 = f32[1,512]{1,0:T(1,128)} custom-call(bf16[640,512]{1,0:T(8,128)(2,1)S(1)} %get-tuple-element.9.design_ref, f32[640,512]{1,0:T(8,128)S(1)} %get-tuple-element.12.phase_ref, f32[640,512]{1,0:T(8,128)S(1)} %get-tuple-element.13.quality_ref, bf16[512,512]{1,0:T(8,128)(2,1)S(1)} %get-tuple-element.14.parts_ref), custom_call_target="tpu_custom_call" | custom-call | tf_op jit(solution)/shard_map/misfit/pallas_call | solution.py:236
  54.2 5.9 %collective-permute-done = f32[2,150]{1,0:T(2,128)S(1)} collective-permute-done((f32[2,150]{1,0:T(2,128)S(1)}, f32[2,150]{1,0:T(2,128)S(1)}, u32[]{:S(2)}, u32[]{:S(2)}) %collective-permute-start) | collective-permute-done | bytes 1232 | tf_op jit(solution)/shard_map/ppermute | solution.py:34
  60.0 0.6 add_bitcast_fusion
  (1 shorter events, 0.0 us)
Async XLA Ops:
  2.5 45.0 %copy-start = (bf16[150,640]{1,0:T(8,128)(2,1)S(1)}, bf16[150,640]{1,0:T(8,128)(2,1)}, u32[]{:S(2)}) copy-start(bf16[150,640]{1,0:T(8,128)(2,1)} %inverse_ref.1) | copy-start | bytes 576004
  2.6 45.0 %copy-start.1 = (s32[1,512]{1,0:T(1,128)S(1)}, s32[1,512]{1,0:T(1,128)}, u32[]{:S(2)}) copy-start(s32[1,512]{1,0:T(1,128)} %footprint_ref.1) | copy-start | bytes 6148
  50.9 9.1 %collective-permute-start = (f32[2,150]{1,0:T(2,128)S(1)}, f32[2,150]{1,0:T(2,128)S(1)}, u32[]{:S(2)}, u32[]{:S(2)}) collective-permute-start(f32[2,150]{1,0:T(2,128)S(1)} %slice.7), channel_id=1, source_target_pairs={{0,1},{1,2},{2,3},{3,4},{4,5},{5,6},{6,7},{7,8},{8,9},{9,10},{10,1... | collective-permute-start | bytes 3608 | tf_op jit(solution)/shard_map/ppermute | solution.py:34
